TPU v7x, 128 devices: a whole 4x4x4 slice. The times are simulated.
128 devices in a mesh: row: 8 (over y, core), col: 16 (over z, x).
Axes of the slice: x: 4, y: 4, z: 4, core: 2. Of those that a mesh axis runs over, the one named last changes fastest.
Arguments:
- near_blocks: bfloat16 [256, 16, 512, 512], P(('row', 'col')), may hold values from -2 to 9, as said below
- leaf_basis: bfloat16 [256, 512, 512], P(('row', 'col')), may hold values from -1 to 2, as said below
- near_cols: int32 [256, 16], P(('row', 'col')), may hold values from 0 to 255, as said below
- near_count: int32 [256], P(('row', 'col')), may hold values from 1 to 16, as said below
- children: int32 [128, 2], replicated, may hold values from 0 to 255, as said below
- parent_basis: bfloat16 [128, 256, 256], P(('row', 'col')), may hold values from -1 to 2, as said below
- far_coupling: float32 [128, 128, 128], P(('row', 'col')), may hold values from -0.25 to 0.25
Outputs:
- leaf_factor: float32 [256, 384, 384], P(('row', 'col'))
- near_schur: float32 [256, 16, 128, 128], P(('row', 'col'))
- top_factor: float32 [128, 128, 128], P(('row', 'col'))
- top_schur: float32 [128, 128, 128], P(('row', 'col'))
Inputs may be any that keep to these rules, and one draw needn't show every extreme that they name: near_cols[i, 0] = i; for 1 <= t < near_count[i] the entries near_cols[i, t] are distinct leaves other than i of i's group, the leaves 32 * g to 32 * g + 31 with g = i // 32; slots t >= near_count[i] hold i. `near_count`: some leaf has 16 live slots. Parent p belongs to group g = 2 * p // 32; children[p, 0] is a leaf of group g and children[p, 1] a leaf of group g + 1 - 2 * (g % 2); every leaf is a child of exactly one parent. near_blocks[i, 0] is symmetric positive definite. `leaf_basis`: each basis is nonsingular. `parent_basis`: each basis is nonsingular.
All inputs are finite; a program needn't handle non-finite values.
Results may differ from a plain program's by a relative error of at most 0.0015.
Values may be sent and summed in bfloat16 or wider, within the bound.
No kernel may reach another device: no remote copies, remote signals or barrier semaphores. Data moves between devices by JAX's collectives and lax.ppermute only.
A program may use at most 192 MiB of HBM per device.

v0:
```python
from functools import partial

import jax
import jax.numpy as jnp
from jax import lax
from jax.experimental import pallas as pl
from jax.experimental.pallas import tpu as pltpu
from jax.sharding import PartitionSpec as P

F32 = jnp.float32
BF16 = jnp.bfloat16
LANE = 128
SUB = 8
HBM = pl.BlockSpec(memory_space=pltpu.HBM)
VMEM = pl.BlockSpec(memory_space=pltpu.VMEM)
SMEM = pl.BlockSpec(memory_space=pltpu.SMEM)
LARGE = pltpu.CompilerParams(vmem_limit_bytes=60 << 20)
STEP = 4


def guess(us):
    return pl.CostEstimate(flops=int(us * 1e9), bytes_accessed=0, transcendentals=0)


def split2(x):
    hi = x.astype(BF16)
    lo = (x - hi.astype(F32)).astype(BF16)
    return hi, lo


def dot(a, b):
    return jnp.dot(a, b, preferred_element_type=F32)


def dot_first(a, b):
    return lax.dot_general(a, b, (((0,), (0,)), ((), ())), preferred_element_type=F32)


def mul3(a, b, op=dot):
    ah, al = split2(a)
    bh, bl = split2(b)
    return op(ah, bh) + (op(ah, bl) + op(al, bh))


def spread(row):
    return jnp.broadcast_to(row, (SUB, row.shape[1]))


def lower_inverse(work, inv):
    n = LANE
    groups = 2
    width = groups * SUB
    row = lax.broadcasted_iota(jnp.int32, (n, n), 0)
    col = lax.broadcasted_iota(jnp.int32, (n, n), 1)
    eye = jnp.where(row == col, 1.0, 0.0).astype(F32)
    sub = lax.broadcasted_iota(jnp.int32, (SUB, n), 0)
    for t in inv:
        t[...] = eye
    for k in range(0, n, width):
        panels = []
        for a, t in zip(work, inv):
            pa = [a[k + g * SUB : k + (g + 1) * SUB, :] for g in range(groups)]
            pt = [t[k + g * SUB : k + (g + 1) * SUB, :] for g in range(groups)]
            cols = [
                [jnp.broadcast_to(pa[g][:, k + j : k + j + 1], (SUB, n)) for j in range((g + 1) * SUB)]
                for g in range(groups)
            ]
            panels.append((pa, pt, cols))
        for j in range(width):
            own, jj = divmod(j, SUB)
            for pa, pt, cols in panels:
                r = lax.rsqrt(spread(cols[own][j][jj : jj + 1]))
                r2 = r * r
                ra = spread(pa[own][jj : jj + 1]) * r
                rt = spread(pt[own][jj : jj + 1]) * r
                elems = {}
                for g in range(own, groups):
                    for m in range(max(j + 1, g * SUB), (g + 1) * SUB):
                        elems[m] = spread(cols[g][j][m - g * SUB : m - g * SUB + 1])
                for g in range(own, groups):
                    base = cols[g][j]
                    for m in range(j + 1, (g + 1) * SUB):
                        cols[g][m] = cols[g][m] - (base * elems[m]) * r2
                    c = base * r
                    if g == own:
                        c = jnp.where(sub > jj, c, 0.0)
                        pa[g] = jnp.where(sub == jj, ra, pa[g] - c * ra)
                        pt[g] = jnp.where(sub == jj, rt, pt[g] - c * rt)
                    else:
                        pa[g] = pa[g] - c * ra
                        pt[g] = pt[g] - c * rt
        for (pa, pt, _), a, t in zip(panels, work, inv):
            a_rows = jnp.concatenate(pa, axis=0)
            t_rows = jnp.concatenate(pt, axis=0)
            a[k : k + width, :] = a_rows
            t[k : k + width, :] = t_rows
            if k + width < n:
                hi, lo = split2(jnp.concatenate([a_rows, t_rows], axis=1))
                left = jnp.concatenate([hi[:, :n], hi[:, :n], lo[:, :n], lo[:, :n]], axis=0)
                right = jnp.concatenate([hi, lo, hi, lo], axis=0)
                upd = dot_first(left, right)
                a[k + width :, :] = a[k + width :, :] - upd[k + width :, :n]
                t[k + width :, :] = t[k + width :, :] - upd[k + width :, n:]


def pack_symmetric(m):
    n = LANE
    row = lax.broadcasted_iota(jnp.int32, (n, n), 0)
    col = lax.broadcasted_iota(jnp.int32, (n, n), 1)
    m = jnp.where(row >= col, m, m.T)
    hi = m.astype(BF16).astype(F32)
    lo = m - hi
    last = jnp.sum(jnp.where(row == col, lo, 0.0), axis=0, keepdims=True)
    body = jnp.where(row >= col, hi, lo)
    return jnp.concatenate([body, jnp.broadcast_to(last, (16, n))], axis=0).astype(BF16)


def unpack_symmetric(packed):
    n = LANE
    row = lax.broadcasted_iota(jnp.int32, (n, n), 0)
    col = lax.broadcasted_iota(jnp.int32, (n, n), 1)
    packed = packed.astype(F32)
    body = packed[:n]
    other = body.T
    last = jnp.broadcast_to(packed[n : n + 1], (n, n))
    return jnp.where(row == col, body + last, body + other)


def diag_kernel(a_ref, u_ref, factor_ref, schur_ref, *refs):
    pays, (w_ref, t_ref) = refs[:-2], refs[-2:]
    leaves = u_ref.shape[0]
    size = u_ref.shape[1]
    n = LANE
    blocks = size // n - 1
    red = blocks * n
    row = lax.broadcasted_iota(jnp.int32, (n, n), 0)
    col = lax.broadcasted_iota(jnp.int32, (n, n), 1)
    upper = row <= col
    for i in range(leaves):
        u = u_ref[i]
        hh, hl = split2(dot(a_ref[i, 0], u))
        w_ref[i] = dot_first(u, hh) + dot_first(u, hl)
    for b in range(blocks):
        lo, hi = b * n, (b + 1) * n
        lower_inverse(
            [w_ref.at[i, lo:hi, lo:hi] for i in range(leaves)],
            [t_ref.at[i, b] for i in range(leaves)],
        )
        for i in range(leaves):
            x = mul3(t_ref[i, b], w_ref[i, lo:hi, hi:])
            w_ref[i, lo:hi, hi:] = x
            xh, xl = split2(x)
            w_ref[i, hi:, hi:] = w_ref[i, hi:, hi:] - (
                dot_first(xh, xh) + (dot_first(xh, xl) + dot_first(xl, xh))
            )
    for i in range(leaves):
        schur = w_ref[i, red:, red:]
        schur_ref[i] = schur
        pays[i][:size, :] = u_ref[i, :, red:]
        pays[i][2 * size :, :] = pack_symmetric(schur)
        piv = [None] * blocks
        for b in reversed(range(blocks)):
            lo, hi = b * n, (b + 1) * n
            y = w_ref[i, lo:hi, red:]
            if b + 1 < blocks:
                y = y - mul3(w_ref[i, lo:hi, hi:red], jnp.concatenate(piv[b + 1 :], axis=0))
            piv[b] = mul3(t_ref[i, b], y, dot_first)
        ph, plo = split2(jnp.concatenate(piv, axis=0))
        ur = u_ref[i, :, :red]
        pays[i][size : 2 * size, :] = (dot(ur, ph) + dot(ur, plo)).astype(BF16)
        for b in range(blocks):
            for c in range(blocks):
                if c < b:
                    blk = w_ref[i, c * n : (c + 1) * n, b * n : (b + 1) * n].T
                elif c == b:
                    blk = jnp.where(upper, w_ref[i, b * n : (b + 1) * n, b * n : (b + 1) * n], 0.0).T
                else:
                    blk = jnp.zeros((n, n), F32)
                factor_ref[i, b * n : (b + 1) * n, c * n : (c + 1) * n] = blk


def diag_part(near_blocks, leaf_basis):
    leaves, size, _ = leaf_basis.shape
    red = size - LANE
    rows = 2 * size + LANE + 16
    return pl.pallas_call(
        diag_kernel,
        grid=(1,),
        in_specs=[
            pl.BlockSpec((leaves, 1, size, size), lambda g: (0, 0, 0, 0)),
            pl.BlockSpec((leaves, size, size), lambda g: (0, 0, 0)),
        ],
        out_specs=[
            pl.BlockSpec((leaves, red, red), lambda g: (0, 0, 0)),
            pl.BlockSpec((leaves, LANE, LANE), lambda g: (0, 0, 0)),
        ]
        + [pl.BlockSpec((rows, LANE), lambda g: (0, 0))] * leaves,
        out_shape=[
            jax.ShapeDtypeStruct((leaves, red, red), F32),
            jax.ShapeDtypeStruct((leaves, LANE, LANE), F32),
        ]
        + [jax.ShapeDtypeStruct((rows, LANE), BF16)] * leaves,
        scratch_shapes=[
            pltpu.VMEM((leaves, size, size), F32),
            pltpu.VMEM((leaves, size // LANE - 1, LANE, LANE), F32),
        ],
        compiler_params=LARGE,
        cost_estimate=guess(26),
        name="diag",
    )(near_blocks, leaf_basis)


def pick_kernel(where_ref, *refs):
    pieces, (first_ref, second_ref, sem) = refs[:-3], refs[-3:]
    rows = first_ref.shape[0]
    half = len(pieces) // 2
    for out, dst in enumerate((first_ref, second_ref)):
        base = 0
        for p, piece in enumerate(pieces):
            if p == half:
                base = 0
            count = piece.shape[0]
            leaf = 0 if p < half else 1
            slot = where_ref[2 * out + 1] - base

            @pl.when((where_ref[2 * out] == leaf) & (slot >= 0) & (slot < count))
            def _(piece=piece, slot=slot, dst=dst, out=out):
                at = jnp.clip(slot, 0, piece.shape[0] - 1)
                pltpu.make_async_copy(piece.at[at, pl.ds(piece.shape[1] - rows, rows)], dst, sem.at[out]).start()

            base += count
    for out, dst in enumerate((first_ref, second_ref)):
        pltpu.make_async_copy(pieces[0].at[0, pl.ds(pieces[0].shape[1] - rows, rows)], dst, sem.at[out]).wait()


def pick_part(where, pieces):
    rows = LANE + 16
    shape = jax.ShapeDtypeStruct((rows, LANE), BF16)
    return pl.pallas_call(
        pick_kernel,
        in_specs=[SMEM] + [HBM] * len(pieces),
        out_shape=[shape, shape],
        scratch_shapes=[pltpu.SemaphoreType.DMA((2,))],
        name="pick",
    )(where, *pieces)


def own_kernel(cnt_ref, a_hbm, *refs):
    pays, (g_hbm, a_buf, g_buf, left_ref, a_sem, g_sem) = refs[:-6], refs[-6:]
    leaves, slots, size, _ = a_hbm.shape

    def load(i, t):
        return pltpu.make_async_copy(a_hbm.at[i, t], a_buf.at[i, t], a_sem.at[i, t])

    def save(i, t):
        return pltpu.make_async_copy(g_buf.at[i, t], g_hbm.at[i, t], g_sem.at[i, t])

    for i in range(leaves):
        lax.fori_loop(1, cnt_ref[i], lambda t, _, i=i: load(i, t).start(), None)
    for i in range(leaves):
        left_ref[i, :LANE, :] = pays[i][:size].T
        left_ref[i, LANE:, :] = pays[i][size : 2 * size].T
    for i in range(leaves):

        def some(c, _, i=i):
            for t in [c * STEP + u for u in range(STEP)]:

                @pl.when((t > 0) & (t < cnt_ref[i]))
                def _(t=t):
                    load(i, t).wait()

            for t in [c * STEP + u for u in range(STEP)]:
                g = dot(left_ref[i], a_buf[i, t])
                g_s = g[:LANE]
                hi, lo = split2(g_s - g[LANE:])
                g_buf[i, t, 0] = hi
                g_buf[i, t, 1] = lo
                g_buf[i, t, 2] = g_s.astype(BF16)
            for t in [c * STEP + u for u in range(STEP)]:

                @pl.when((t > 0) & (t < cnt_ref[i]))
                def _(t=t):
                    save(i, t).start()

        lax.fori_loop(0, (cnt_ref[i] + (STEP - 1)) // STEP, some, None)
    for i in range(leaves):
        lax.fori_loop(1, cnt_ref[i], lambda t, _, i=i: save(i, t).wait(), None)


def own_part(counts, near_blocks, pays):
    leaves, slots, size, _ = near_blocks.shape
    shape = (leaves, slots, 3, LANE, size)
    return pl.pallas_call(
        own_kernel,
        in_specs=[SMEM, HBM] + [VMEM] * len(pays),
        out_specs=HBM,
        out_shape=jax.ShapeDtypeStruct(shape, BF16),
        scratch_shapes=[
            pltpu.VMEM(near_blocks.shape, BF16),
            pltpu.VMEM(shape, BF16),
            pltpu.VMEM((leaves, 2 * LANE, size), BF16),
            pltpu.SemaphoreType.DMA((leaves, slots)),
            pltpu.SemaphoreType.DMA((leaves, slots)),
        ],
        compiler_params=LARGE,
        cost_estimate=guess(8),
        name="own",
    )(counts, near_blocks, *pays)


def near_kernel(off_ref, spot_ref, cnt_ref, schur_ref, g_hbm, *refs):
    pieces, (out_ref, g_buf, r_buf, g_sem, r_sem) = refs[:-5], refs[-5:]
    leaves, slots = out_ref.shape[:2]
    rows = r_buf.shape[2]
    half = len(pieces) // 2
    count = pieces[0].shape[0]

    def load(i, t):
        return pltpu.make_async_copy(g_hbm.at[i, t], g_buf.at[i, t], g_sem.at[i, t])

    def fetch(i, t, piece, at):
        return pltpu.make_async_copy(piece.at[at, pl.ds(0, rows)], r_buf.at[i, t], r_sem.at[i, t])

    for i in range(leaves):

        def begin(t, _, i=i):
            load(i, t).start()
            at = i * slots + t
            spot = spot_ref[at]
            number = lax.rem(off_ref[at], 2) * half + lax.div(spot, count)
            for p, piece in enumerate(pieces):

                @pl.when(number == p)
                def _(piece=piece):
                    fetch(i, t, piece, lax.rem(spot, count)).start()

        lax.fori_loop(1, cnt_ref[i], begin, None)
    size = rows // 2
    for i in range(leaves):

        def some(c, _, i=i):
            for t in [c * STEP + u for u in range(STEP)]:

                @pl.when((t > 0) & (t < cnt_ref[i]))
                def _(t=t):
                    load(i, t).wait()
                    fetch(i, t, pieces[0], 0).wait()

            for t in [c * STEP + u for u in range(STEP)]:
                s_j = r_buf[i, t, :size]
                both = dot(g_buf[i, t, :2].reshape(2 * LANE, size), s_j)
                value = both[:LANE] + both[LANE:] - dot(g_buf[i, t, 2], r_buf[i, t, size:])
                out_ref[i, t] = jnp.where(t < cnt_ref[i], value, 0.0)

        def dead(t, _, i=i):
            out_ref[i, t] = jnp.zeros(out_ref.shape[2:], F32)

        steps = (cnt_ref[i] + (STEP - 1)) // STEP
        lax.fori_loop(0, steps, some, None)
        lax.fori_loop(steps * STEP, slots, dead, None)
        out_ref[i, 0] = schur_ref[i]


def near_part(offsets, spots, counts, schur, g, pieces):
    leaves, slots, _, _, size = g.shape
    return pl.pallas_call(
        near_kernel,
        in_specs=[SMEM, SMEM, SMEM, VMEM, HBM] + [HBM] * len(pieces),
        out_specs=VMEM,
        out_shape=jax.ShapeDtypeStruct((leaves, slots, LANE, LANE), F32),
        scratch_shapes=[
            pltpu.VMEM(g.shape, BF16),
            pltpu.VMEM((leaves, slots, 2 * size, LANE), BF16),
            pltpu.SemaphoreType.DMA((leaves, slots)),
            pltpu.SemaphoreType.DMA((leaves, slots)),
        ],
        compiler_params=LARGE,
        cost_estimate=guess(6),
        name="near",
    )(offsets, spots, counts, schur, g, *pieces)


def top_kernel(first_ref, second_ref, far_ref, v_ref, factor_ref, top_ref, w_ref, t_ref):
    n = LANE
    row = lax.broadcasted_iota(jnp.int32, (n, n), 0)
    col = lax.broadcasted_iota(jnp.int32, (n, n), 1)
    far = far_ref[0]
    merged = jnp.concatenate(
        [
            jnp.concatenate([unpack_symmetric(first_ref[...]), far], axis=1),
            jnp.concatenate([far.T, unpack_symmetric(second_ref[...])], axis=1),
        ],
        axis=0,
    )
    v = v_ref[0]
    mh, ml = split2(merged)
    hh, hl = split2(dot(mh, v) + dot(ml, v))
    p = dot_first(v, hh) + dot_first(v, hl)
    w_ref[...] = p[:n, :n]
    lower_inverse([w_ref], [t_ref])
    x = mul3(t_ref[...], p[:n, n:])
    top_ref[0] = p[n:, n:] - mul3(x, x, dot_first)
    factor_ref[0] = jnp.where(row <= col, w_ref[...], 0.0).T


def top_part(first, second, far, basis):
    shape = jax.ShapeDtypeStruct((1, LANE, LANE), F32)
    return pl.pallas_call(
        top_kernel,
        out_shape=[shape, shape],
        scratch_shapes=[pltpu.VMEM((LANE, LANE), F32), pltpu.VMEM((LANE, LANE), F32)],
        compiler_params=LARGE,
        cost_estimate=guess(8),
        name="top",
    )(first, second, far, basis)


def shifted(x, side, step_z, step_x):
    route = []
    for i in range(side * side):
        z, w = divmod(i, side)
        route.append((i, (z + step_z) % side * side + (w + step_x) % side))
    return lax.ppermute(x, "col", route)


def ways(side):
    def along_x(v, d):
        return shifted(v, side, 0, d)

    def along_z(v, d):
        return shifted(v, side, d, 0)

    return along_x, along_z


def near_ring(x, shift):
    return shift(x, 1), shift(x, -1)


def place(delta):
    return jnp.where(delta == 0, 0, jnp.where(delta == 3, 1, jnp.where(delta == 1, 2, 3)))


def local(near_blocks, leaf_basis, near_cols, near_count, children, parent_basis, far_coupling):
    leaves, slots = near_cols.shape
    row_index = lax.axis_index("row")
    col_index = lax.axis_index("col")
    row_count = lax.axis_size("row")
    col_count = lax.axis_size("col")
    side = 4
    group_size = leaves * col_count
    group_base = row_index * group_size

    def spot(offset):
        device = offset // 2
        z = place((device // side - col_index // side) % side)
        x = place((device % side - col_index % side) % side)
        return jnp.where(offset % 2 == 0, z * side + x, x * side + z)

    partner_row = row_index + 1 - 2 * (row_index % 2)
    parent_id = row_index * col_count + col_index
    partner_parent = partner_row * col_count + col_index
    child = jnp.stack([children[parent_id, 0], children[partner_parent, 1]]) - group_base
    where = jnp.stack([child % 2, spot(child)], axis=1).reshape(-1)
    offsets = (near_cols - group_base).reshape(-1)
    spots = spot(offsets)

    hold = lax.optimization_barrier
    first_way, second_way = ways(side)
    orders = ((first_way, second_way), (second_way, first_way))
    factors, schur, *pays = diag_part(near_blocks, leaf_basis)
    near = [near_ring(pays[k], orders[k][0]) for k in range(2)]
    low = [jnp.stack([pays[k], near[k][0]]) for k in range(2)]
    low_far = [near_ring(low[k], orders[k][1]) for k in range(2)]
    far = [orders[0][0](near[0][0], 1), orders[1][0](near[1][1], -1)]
    own_pays, _ = hold((pays, low))
    g = own_part(near_count, near_blocks, own_pays)
    g, ahead, far = hold((g, [near[k][1] for k in range(2)], far))
    high = [jnp.stack([ahead[k], far[k]]) for k in range(2)]
    high_far = [near_ring(high[k], orders[k][1]) for k in range(2)]
    pieces = []
    for k in range(2):
        shift = orders[k][1]
        pieces += [low[k], high[k], low_far[k][0], high_far[k][0], low_far[k][1], high_far[k][1]]
        pieces += [shift(low_far[k][0], 1), shift(high_far[k][1], -1)]
    first, outgoing = pick_part(where, pieces)
    second = lax.ppermute(outgoing, "row", [(r, r ^ 1) for r in range(row_count)])
    near_schur = near_part(offsets, spots, near_count, schur, g, pieces)
    top_factor, top_schur = top_part(first, second, far_coupling, parent_basis)
    return factors, near_schur, top_factor, top_schur


def solution(mesh):
    both = ("row", "col")
    return jax.shard_map(
        local,
        mesh=mesh,
        in_specs=(P(both), P(both), P(both), P(both), P(), P(both), P(both)),
        out_specs=(P(both), P(both), P(both), P(both)),
        check_vma=False,
    )
```

profile of v0, /device:TPU:1, one launch (start us, length us, event | category | flops | bytes accessed | tf_op | source)
XLA Modules:
  0.0 108.5 jit_solution(13656663661656878959)
XLA Ops:
  0.6 21.6 %diag.1 = (f32[2,384,384]{2,1,0:T(8,128)}, f32[2,128,128]{2,1,0:T(8,128)}, bf16[1168,128]{1,0:T(8,128)(2,1)}, bf16[1168,128]{1,0:T(8,128)(2,1)}) custom-call(bf16[2,16,512,512]{3,2,1,0:T(8,128)(2,1)} %a_hbm.1, bf16[2,512,512]{2,1,0:T(8,128)(2,1)} %u_ref.1), custom_call_target="tpu_custom_call" | custom-call | flops 25999998976 | tf_op jit(solution)/shard_map/diag/pallas_call | solution.py:186
  22.2 2.0 %collective-permute-start = (bf16[1168,128]{1,0:T(8,128)(2,1)}, bf16[1168,128]{1,0:T(8,128)(2,1)S(1)}, u32[]{:S(2)}, u32[]{:S(2)}) collective-permute-start(bf16[1168,128]{1,0:T(8,128)(2,1)} %get-tuple-element.23.refs_0_), channel_id=1, source_target_pairs={{0,1},{1,2},{2,3},{3,0},{4,5},{5,6},{6,7},{7,4},{8,9},{9,10},{10,1... | collective-permute-start | bytes 897032 | tf_op jit(solution)/shard_map/ppermute | solution.py:423
  24.2 1.6 %collective-permute-start.1 = (bf16[1168,128]{1,0:T(8,128)(2,1)}, bf16[1168,128]{1,0:T(8,128)(2,1)S(1)}, u32[]{:S(2)}, u32[]{:S(2)}) collective-permute-start(bf16[1168,128]{1,0:T(8,128)(2,1)} %get-tuple-element.24.refs_1_), channel_id=1, source_target_pairs={{0,4},{1,5},{2,6},{3,7},{4,8},{5,9},{6,10},{7,11},{8,12},{9,13},{1... | collective-permute-start | bytes 897032 | tf_op jit(solution)/shard_map/ppermute | solution.py:423
  25.9 1.5 %collective-permute-start.2 = (bf16[1168,128]{1,0:T(8,128)(2,1)}, bf16[1168,128]{1,0:T(8,128)(2,1)S(1)}, u32[]{:S(2)}, u32[]{:S(2)}) collective-permute-start(bf16[1168,128]{1,0:T(8,128)(2,1)} %get-tuple-element.23.refs_0_), channel_id=1, source_target_pairs={{0,3},{1,0},{2,1},{3,2},{4,7},{5,4},{6,5},{7,6},{8,11},{9,8},{10,9... | collective-permute-start | bytes 897032 | tf_op jit(solution)/shard_map/ppermute | solution.py:423
  27.3 2.1 %collective-permute-start.3 = (bf16[1168,128]{1,0:T(8,128)(2,1)}, bf16[1168,128]{1,0:T(8,128)(2,1)S(1)}, u32[]{:S(2)}, u32[]{:S(2)}) collective-permute-start(bf16[1168,128]{1,0:T(8,128)(2,1)} %get-tuple-element.24.refs_1_), channel_id=1, source_target_pairs={{0,12},{1,13},{2,14},{3,15},{4,0},{5,1},{6,2},{7,3},{8,4},{9,5},{1... | collective-permute-start | bytes 897032 | tf_op jit(solution)/shard_map/ppermute | solution.py:423
  29.5 2.6 %collective-permute-done = bf16[1168,128]{1,0:T(8,128)(2,1)S(1)} collective-permute-done((bf16[1168,128]{1,0:T(8,128)(2,1)}, bf16[1168,128]{1,0:T(8,128)(2,1)S(1)}, u32[]{:S(2)}, u32[]{:S(2)}) %collective-permute-start) | collective-permute-done | bytes 299040 | tf_op jit(solution)/shard_map/ppermute | solution.py:423
  32.1 1.0 pad_maximum_fusion.refs_0_
  33.1 0.0 copy-start
  33.1 4.1 %collective-permute-start.8 = (bf16[2,1168,128]{2,1,0:T(8,128)(2,1)S(1)}, bf16[2,1168,128]{2,1,0:T(8,128)(2,1)S(1)}, u32[]{:S(2)}, u32[]{:S(2)}) collective-permute-start(bf16[2,1168,128]{2,1,0:T(8,128)(2,1)S(1)} %pad_maximum_fusion.refs_0_), channel_id=1, source_target_pairs={{0,12},{1,13},{2,14},{3,15},{4,0},{5,1},{6,2},{7,3},{8,4},{9,5},{1... | collective-permute-start | bytes 1794056 | tf_op jit(solution)/shard_map/ppermute | solution.py:423
  37.3 0.0 collective-permute-start.6
  37.3 0.0 collective-permute-done.1
  37.3 1.0 pad_maximum_fusion.1.refs_8_
  38.3 0.0 copy-start.1
  38.3 0.0 copy-start.8
  38.3 0.0 copy-start.9
  38.3 0.1 collective-permute-start.4
  38.4 0.0 collective-permute-done.3
  38.4 2.7 %collective-permute-start.5 = (bf16[1168,128]{1,0:T(8,128)(2,1)S(1)}, bf16[1168,128]{1,0:T(8,128)(2,1)S(1)}, u32[]{:S(2)}, u32[]{:S(2)}) collective-permute-start(bf16[1168,128]{1,0:T(8,128)(2,1)S(1)} %collective-permute-done.3), channel_id=1, source_target_pairs={{0,12},{1,13},{2,14},{3,15},{4,0},{5,1},{6,2},{7,3},{8,4},{9,5},{1... | collective-permute-start | bytes 897032 | tf_op jit(solution)/shard_map/ppermute | solution.py:423
  41.2 6.2 %own.1.g_hbm = bf16[2,16,3,128,512]{4,3,2,1,0:T(8,128)(2,1)} custom-call(s32[2]{0:T(128)} %cnt_ref.3, bf16[2,16,512,512]{3,2,1,0:T(8,128)(2,1)} %a_hbm.1, bf16[1168,128]{1,0:T(8,128)(2,1)} %get-tuple-element.23.refs_0_, bf16[1168,128]{1,0:T(8,128)(2,1)} %get-tuple-element.24.refs_1_), custom_call_target="tpu_custom_call" | custom-call | flops 8000000000 | tf_op jit(solution)/shard_map/own/pallas_call | solution.py:293
  47.4 0.0 copy-done
  47.4 0.0 collective-permute-done.2
  47.4 2.5 %collective-permute-start.14 = (bf16[2,1168,128]{2,1,0:T(8,128)(2,1)S(1)}, bf16[2,1168,128]{2,1,0:T(8,128)(2,1)}, u32[]{:S(2)}, u32[]{:S(2)}) collective-permute-start(bf16[2,1168,128]{2,1,0:T(8,128)(2,1)S(1)} %pad_maximum_fusion.1.refs_8_), channel_id=1, source_target_pairs={{0,3},{1,0},{2,1},{3,2},{4,7},{5,4},{6,5},{7,6},{8,11},{9,8},{10,9... | collective-permute-start | bytes 1794056 | tf_op jit(solution)/shard_map/ppermute | solution.py:423
  50.0 0.0 collective-permute-done.4
  50.0 0.0 copy-done.1
  50.0 0.0 collective-permute-start.12
  50.0 4.9 %collective-permute-done.5 = bf16[1168,128]{1,0:T(8,128)(2,1)S(1)} collective-permute-done((bf16[1168,128]{1,0:T(8,128)(2,1)S(1)}, bf16[1168,128]{1,0:T(8,128)(2,1)S(1)}, u32[]{:S(2)}, u32[]{:S(2)}) %collective-permute-start.5) | collective-permute-done | bytes 299040 | tf_op jit(solution)/shard_map/ppermute | solution.py:423
  54.9 0.1 pad_maximum_fusion.3.refs_9_
  55.0 0.0 copy-start.2
  55.0 1.4 %collective-permute-start.15 = (bf16[2,1168,128]{2,1,0:T(8,128)(2,1)S(1)}, bf16[2,1168,128]{2,1,0:T(8,128)(2,1)}, u32[]{:S(2)}, u32[]{:S(2)}) collective-permute-start(bf16[2,1168,128]{2,1,0:T(8,128)(2,1)S(1)} %pad_maximum_fusion.3.refs_9_), channel_id=1, source_target_pairs={{0,3},{1,0},{2,1},{3,2},{4,7},{5,4},{6,5},{7,6},{8,11},{9,8},{10,9... | collective-permute-start | bytes 1794056 | tf_op jit(solution)/shard_map/ppermute | solution.py:423
  56.3 0.1 pad_maximum_fusion.2.refs_1_
  56.4 0.0 collective-permute-done.8.refs_4_
  56.4 0.0 copy-start.4
  56.4 0.2 collective-permute-start.13
  56.7 0.0 collective-permute-done.6.refs_2_
  56.7 3.5 %collective-permute-start.9 = (bf16[2,1168,128]{2,1,0:T(8,128)(2,1)S(1)}, bf16[2,1168,128]{2,1,0:T(8,128)(2,1)S(1)}, u32[]{:S(2)}, u32[]{:S(2)}) collective-permute-start(bf16[2,1168,128]{2,1,0:T(8,128)(2,1)S(1)} %pad_maximum_fusion.2.refs_1_), channel_id=1, source_target_pairs={{0,12},{1,13},{2,14},{3,15},{4,0},{5,1},{6,2},{7,3},{8,4},{9,5},{1... | collective-permute-start | bytes 1794056 | tf_op jit(solution)/shard_map/ppermute | solution.py:423
  60.2 0.6 constant_dynamic-slice_fusion.1
  60.8 0.2 collective-permute-done.14.refs_12_
  61.0 0.0 collective-permute-start.7
  61.0 3.2 %collective-permute-done.12.refs_10_ = bf16[2,1168,128]{2,1,0:T(8,128)(2,1)} collective-permute-done((bf16[2,1168,128]{2,1,0:T(8,128)(2,1)S(1)}, bf16[2,1168,128]{2,1,0:T(8,128)(2,1)}, u32[]{:S(2)}, u32[]{:S(2)}) %collective-permute-start.12) | collective-permute-done | bytes 598048 | tf_op jit(solution)/shard_map/ppermute | solution.py:423
  64.2 0.0 collective-permute-start.10
  64.2 9.6 %collective-permute-done.15.refs_13_ = bf16[2,1168,128]{2,1,0:T(8,128)(2,1)} collective-permute-done((bf16[2,1168,128]{2,1,0:T(8,128)(2,1)S(1)}, bf16[2,1168,128]{2,1,0:T(8,128)(2,1)}, u32[]{:S(2)}, u32[]{:S(2)}) %collective-permute-start.15) | collective-permute-done | bytes 598048 | tf_op jit(solution)/shard_map/ppermute | solution.py:423
  73.8 0.0 collective-permute-start.16
  73.8 3.2 %collective-permute-done.13.refs_11_ = bf16[2,1168,128]{2,1,0:T(8,128)(2,1)} collective-permute-done((bf16[2,1168,128]{2,1,0:T(8,128)(2,1)S(1)}, bf16[2,1168,128]{2,1,0:T(8,128)(2,1)}, u32[]{:S(2)}, u32[]{:S(2)}) %collective-permute-start.13) | collective-permute-done | bytes 598048 | tf_op jit(solution)/shard_map/ppermute | solution.py:423
  77.0 0.3 collective-permute-start.17
  77.3 0.0 collective-permute-done.9.refs_5_
  77.3 0.0 collective-permute-start.11
  77.3 1.4 %compare_select_fusion.14 = (s32[2,1]{0,1:T(1,128)S(1)}, s32[2,1]{0,1:T(1,128)S(1)}) fusion(s32[]{:T(128)S(6)} %select_n.230, s32[]{:T(128)S(6)} %select_n.224, s32[]{:T(128)S(6)} %mul.38, s32[1,1]{0,1:T(1,128)} %get-tuple-element.37, s32[1,1]{0,1:T(1,128)} %get-tuple-element.36), kind=kLoop, calls=%fused_computation.23 | loop fusion | flops 164 | bytes 36 | tf_op jit(solution)/shard_map/jit(_where)/select_n | solution.py:458
  78.8 0.1 copy.11
  78.9 0.6 reshape.310.where_ref
  79.5 0.1 reshape.309.off_ref
  79.6 0.6 compare_select_fusion.21.spot_ref
  80.2 0.0 collective-permute-done.7.refs_3_
  80.2 2.4 %collective-permute-done.10.refs_6_ = bf16[2,1168,128]{2,1,0:T(8,128)(2,1)S(1)} collective-permute-done((bf16[2,1168,128]{2,1,0:T(8,128)(2,1)}, bf16[2,1168,128]{2,1,0:T(8,128)(2,1)S(1)}, u32[]{:S(2)}, u32[]{:S(2)}) %collective-permute-start.10) | collective-permute-done | bytes 598048 | tf_op jit(solution)/shard_map/ppermute | solution.py:423
  82.6 7.6 %collective-permute-done.16.refs_14_ = bf16[2,1168,128]{2,1,0:T(8,128)(2,1)} collective-permute-done((bf16[2,1168,128]{2,1,0:T(8,128)(2,1)}, bf16[2,1168,128]{2,1,0:T(8,128)(2,1)}, u32[]{:S(2)}, u32[]{:S(2)}) %collective-permute-start.16) | collective-permute-done | bytes 598048 | tf_op jit(solution)/shard_map/ppermute | solution.py:423
  90.2 0.0 collective-permute-done.17.refs_15_
  90.2 0.0 collective-permute-done.11.refs_7_
  90.3 2.2 %pick.1 = (bf16[144,128]{1,0:T(8,128)(2,1)}, bf16[144,128]{1,0:T(8,128)(2,1)}) custom-call(s32[4]{0:T(128)} %reshape.310.where_ref, bf16[2,1168,128]{2,1,0:T(8,128)(2,1)} %copy-done, bf16[2,1168,128]{2,1,0:T(8,128)(2,1)} %copy-done.3, bf16[2,1168,128]{2,1,0:T(8,128)(2,1)} %collective-permute-done.6.refs_2_, ...), custom_call_target="tpu_custom_call" | custom-call | tf_op jit(solution)/shard_map/pick/pallas_call | solution.py:239
  92.5 3.2 %collective-permute-start.18 = (bf16[144,128]{1,0:T(8,128)(2,1)}, bf16[144,128]{1,0:T(8,128)(2,1)S(1)}, u32[]{:S(2)}, u32[]{:S(2)}) collective-permute-start(bf16[144,128]{1,0:T(8,128)(2,1)} %get-tuple-element.31), channel_id=1, source_target_pairs={{0,16},{16,0},{32,48},{48,32},{64,80},{80,64},{96,112},{112,96},{1... | collective-permute-start | bytes 110600 | tf_op jit(solution)/shard_map/ppermute | solution.py:487
  95.7 0.0 copy-done.7
  95.7 6.2 %near.1 = f32[2,16,128,128]{3,2,1,0:T(8,128)} custom-call(s32[32]{0:T(128)} %copy-done.7, s32[32]{0:T(128)} %compare_select_fusion.21.spot_ref, s32[2]{0:T(128)} %cnt_ref.3, f32[2,128,128]{2,1,0:T(8,128)} %get-tuple-element.20.schur_ref, bf16[2,16,3,128,512]{4,3,2,1,0:T(8,128)(2,1)} %own.1.g_hbm, bf16[2,1168,128]{2,1,0:T(8,128)(2,1)} %copy-done, ...), custom_call_target="tpu_custom_call" | custom-call | flops 6000000000 | tf_op jit(solution)/shard_map/near/pallas_call | solution.py:366
  101.8 0.0 collective-permute-done.18.second_ref
  101.9 0.0 copy-start.10
  101.9 0.6 copy-done.10
  102.5 6.0 %top.1 = (f32[1,128,128]{2,1,0:T(8,128)}, f32[1,128,128]{2,1,0:T(8,128)}) custom-call(bf16[144,128]{1,0:T(8,128)(2,1)} %get-tuple-element.30.first_ref, bf16[144,128]{1,0:T(8,128)(2,1)} %copy-done.10, f32[1,128,128]{2,1,0:T(8,128)} %far_ref.1, bf16[1,256,256]{2,1,0:T(8,128)(2,1)} %v_ref.1), custom_call_target="tpu_custom_call" | custom-call | flops 8000000000 | tf_op jit(solution)/shard_map/top/pallas_call | solution.py:408
  (13 shorter events, 0.0 us)
Async XLA Ops:
  22.2 9.9 %collective-permute-start = (bf16[1168,128]{1,0:T(8,128)(2,1)}, bf16[1168,128]{1,0:T(8,128)(2,1)S(1)}, u32[]{:S(2)}, u32[]{:S(2)}) collective-permute-start(bf16[1168,128]{1,0:T(8,128)(2,1)} %get-tuple-element.23.refs_0_), channel_id=1, source_target_pairs={{0,1},{1,2},{2,3},{3,0},{4,5},{5,6},{6,7},{7,4},{8,9},{9,10},{10,1... | collective-permute-start | bytes 897032 | tf_op jit(solution)/shard_map/ppermute | solution.py:423
  24.2 13.0 %collective-permute-start.1 = (bf16[1168,128]{1,0:T(8,128)(2,1)}, bf16[1168,128]{1,0:T(8,128)(2,1)S(1)}, u32[]{:S(2)}, u32[]{:S(2)}) collective-permute-start(bf16[1168,128]{1,0:T(8,128)(2,1)} %get-tuple-element.24.refs_1_), channel_id=1, source_target_pairs={{0,4},{1,5},{2,6},{3,7},{4,8},{5,9},{6,10},{7,11},{8,12},{9,13},{1... | collective-permute-start | bytes 897032 | tf_op jit(solution)/shard_map/ppermute | solution.py:423
  25.9 21.6 %collective-permute-start.2 = (bf16[1168,128]{1,0:T(8,128)(2,1)}, bf16[1168,128]{1,0:T(8,128)(2,1)S(1)}, u32[]{:S(2)}, u32[]{:S(2)}) collective-permute-start(bf16[1168,128]{1,0:T(8,128)(2,1)} %get-tuple-element.23.refs_0_), channel_id=1, source_target_pairs={{0,3},{1,0},{2,1},{3,2},{4,7},{5,4},{6,5},{7,6},{8,11},{9,8},{10,9... | collective-permute-start | bytes 897032 | tf_op jit(solution)/shard_map/ppermute | solution.py:423
  27.3 11.1 %collective-permute-start.3 = (bf16[1168,128]{1,0:T(8,128)(2,1)}, bf16[1168,128]{1,0:T(8,128)(2,1)S(1)}, u32[]{:S(2)}, u32[]{:S(2)}) collective-permute-start(bf16[1168,128]{1,0:T(8,128)(2,1)} %get-tuple-element.24.refs_1_), channel_id=1, source_target_pairs={{0,12},{1,13},{2,14},{3,15},{4,0},{5,1},{6,2},{7,3},{8,4},{9,5},{1... | collective-permute-start | bytes 897032 | tf_op jit(solution)/shard_map/ppermute | solution.py:423
  33.1 14.3 %copy-start = (bf16[2,1168,128]{2,1,0:T(8,128)(2,1)}, bf16[2,1168,128]{2,1,0:T(8,128)(2,1)S(1)}, u32[]{:S(2)}) copy-start(bf16[2,1168,128]{2,1,0:T(8,128)(2,1)S(1)} %pad_maximum_fusion.refs_0_) | copy-start | bytes 1794052
  33.1 23.3 %collective-permute-start.8 = (bf16[2,1168,128]{2,1,0:T(8,128)(2,1)S(1)}, bf16[2,1168,128]{2,1,0:T(8,128)(2,1)S(1)}, u32[]{:S(2)}, u32[]{:S(2)}) collective-permute-start(bf16[2,1168,128]{2,1,0:T(8,128)(2,1)S(1)} %pad_maximum_fusion.refs_0_), channel_id=1, source_target_pairs={{0,12},{1,13},{2,14},{3,15},{4,0},{5,1},{6,2},{7,3},{8,4},{9,5},{1... | collective-permute-start | bytes 1794056 | tf_op jit(solution)/shard_map/ppermute | solution.py:423
  37.3 19.4 %collective-permute-start.6 = (bf16[2,1168,128]{2,1,0:T(8,128)(2,1)S(1)}, bf16[2,1168,128]{2,1,0:T(8,128)(2,1)}, u32[]{:S(2)}, u32[]{:S(2)}) collective-permute-start(bf16[2,1168,128]{2,1,0:T(8,128)(2,1)S(1)} %pad_maximum_fusion.refs_0_), channel_id=1, source_target_pairs={{0,4},{1,5},{2,6},{3,7},{4,8},{5,9},{6,10},{7,11},{8,12},{9,13},{1... | collective-permute-start | bytes 1794056 | tf_op jit(solution)/shard_map/ppermute | solution.py:423
  38.3 11.7 %copy-start.1 = (bf16[2,1168,128]{2,1,0:T(8,128)(2,1)}, bf16[2,1168,128]{2,1,0:T(8,128)(2,1)S(1)}, u32[]{:S(2)}) copy-start(bf16[2,1168,128]{2,1,0:T(8,128)(2,1)S(1)} %pad_maximum_fusion.1.refs_8_) | copy-start | bytes 1794052
  38.3 21.9 %copy-start.8 = (s32[128,2]{0,1:T(2,128)S(1)}, s32[128,2]{0,1:T(2,128)}, u32[]{:S(2)}) copy-start(s32[128,2]{0,1:T(2,128)} %param.11) | copy-start | bytes 3076
  38.3 41.2 %copy-start.9 = (s32[2,16]{1,0:T(2,128)S(1)}, s32[2,16]{1,0:T(2,128)}, u32[]{:S(2)}) copy-start(s32[2,16]{1,0:T(2,128)} %param.9) | copy-start | bytes 388
  38.3 11.6 %collective-permute-start.4 = (bf16[1168,128]{1,0:T(8,128)(2,1)S(1)}, bf16[1168,128]{1,0:T(8,128)(2,1)S(1)}, u32[]{:S(2)}, u32[]{:S(2)}) collective-permute-start(bf16[1168,128]{1,0:T(8,128)(2,1)S(1)} %collective-permute-done), channel_id=1, source_target_pairs={{0,1},{1,2},{2,3},{3,0},{4,5},{5,6},{6,7},{7,4},{8,9},{9,10},{10,1... | collective-permute-start | bytes 897032 | tf_op jit(solution)/shard_map/ppermute | solution.py:423
  38.4 16.5 %collective-permute-start.5 = (bf16[1168,128]{1,0:T(8,128)(2,1)S(1)}, bf16[1168,128]{1,0:T(8,128)(2,1)S(1)}, u32[]{:S(2)}, u32[]{:S(2)}) collective-permute-start(bf16[1168,128]{1,0:T(8,128)(2,1)S(1)} %collective-permute-done.3), channel_id=1, source_target_pairs={{0,12},{1,13},{2,14},{3,15},{4,0},{5,1},{6,2},{7,3},{8,4},{9,5},{1... | collective-permute-start | bytes 897032 | tf_op jit(solution)/shard_map/ppermute | solution.py:423
  47.4 13.5 %collective-permute-start.14 = (bf16[2,1168,128]{2,1,0:T(8,128)(2,1)S(1)}, bf16[2,1168,128]{2,1,0:T(8,128)(2,1)}, u32[]{:S(2)}, u32[]{:S(2)}) collective-permute-start(bf16[2,1168,128]{2,1,0:T(8,128)(2,1)S(1)} %pad_maximum_fusion.1.refs_8_), channel_id=1, source_target_pairs={{0,3},{1,0},{2,1},{3,2},{4,7},{5,4},{6,5},{7,6},{8,11},{9,8},{10,9... | collective-permute-start | bytes 1794056 | tf_op jit(solution)/shard_map/ppermute | solution.py:423
  50.0 14.3 %collective-permute-start.12 = (bf16[2,1168,128]{2,1,0:T(8,128)(2,1)S(1)}, bf16[2,1168,128]{2,1,0:T(8,128)(2,1)}, u32[]{:S(2)}, u32[]{:S(2)}) collective-permute-start(bf16[2,1168,128]{2,1,0:T(8,128)(2,1)S(1)} %pad_maximum_fusion.1.refs_8_), channel_id=1, source_target_pairs={{0,1},{1,2},{2,3},{3,0},{4,5},{5,6},{6,7},{7,4},{8,9},{9,10},{10,1... | collective-permute-start | bytes 1794056 | tf_op jit(solution)/shard_map/ppermute | solution.py:423
  55.0 35.3 %copy-start.2 = (bf16[2,1168,128]{2,1,0:T(8,128)(2,1)}, bf16[2,1168,128]{2,1,0:T(8,128)(2,1)S(1)}, u32[]{:S(2)}) copy-start(bf16[2,1168,128]{2,1,0:T(8,128)(2,1)S(1)} %pad_maximum_fusion.3.refs_9_) | copy-start | bytes 1794052
  55.0 18.8 %collective-permute-start.15 = (bf16[2,1168,128]{2,1,0:T(8,128)(2,1)S(1)}, bf16[2,1168,128]{2,1,0:T(8,128)(2,1)}, u32[]{:S(2)}, u32[]{:S(2)}) collective-permute-start(bf16[2,1168,128]{2,1,0:T(8,128)(2,1)S(1)} %pad_maximum_fusion.3.refs_9_), channel_id=1, source_target_pairs={{0,3},{1,0},{2,1},{3,2},{4,7},{5,4},{6,5},{7,6},{8,11},{9,8},{10,9... | collective-permute-start | bytes 1794056 | tf_op jit(solution)/shard_map/ppermute | solution.py:423
  56.4 33.9 %copy-start.3 = (bf16[2,1168,128]{2,1,0:T(8,128)(2,1)}, bf16[2,1168,128]{2,1,0:T(8,128)(2,1)S(1)}, u32[]{:S(2)}) copy-start(bf16[2,1168,128]{2,1,0:T(8,128)(2,1)S(1)} %pad_maximum_fusion.2.refs_1_) | copy-start | bytes 1794052
  56.4 33.9 %copy-start.4 = (bf16[2,1168,128]{2,1,0:T(8,128)(2,1)}, bf16[2,1168,128]{2,1,0:T(8,128)(2,1)S(1)}, u32[]{:S(2)}) copy-start(bf16[2,1168,128]{2,1,0:T(8,128)(2,1)S(1)} %collective-permute-done.8.refs_4_) | copy-start | bytes 1794052
  56.4 20.6 %collective-permute-start.13 = (bf16[2,1168,128]{2,1,0:T(8,128)(2,1)S(1)}, bf16[2,1168,128]{2,1,0:T(8,128)(2,1)}, u32[]{:S(2)}, u32[]{:S(2)}) collective-permute-start(bf16[2,1168,128]{2,1,0:T(8,128)(2,1)S(1)} %pad_maximum_fusion.3.refs_9_), channel_id=1, source_target_pairs={{0,1},{1,2},{2,3},{3,0},{4,5},{5,6},{6,7},{7,4},{8,9},{9,10},{10,1... | collective-permute-start | bytes 1794056 | tf_op jit(solution)/shard_map/ppermute | solution.py:423
  56.7 20.7 %collective-permute-start.9 = (bf16[2,1168,128]{2,1,0:T(8,128)(2,1)S(1)}, bf16[2,1168,128]{2,1,0:T(8,128)(2,1)S(1)}, u32[]{:S(2)}, u32[]{:S(2)}) collective-permute-start(bf16[2,1168,128]{2,1,0:T(8,128)(2,1)S(1)} %pad_maximum_fusion.2.refs_1_), channel_id=1, source_target_pairs={{0,12},{1,13},{2,14},{3,15},{4,0},{5,1},{6,2},{7,3},{8,4},{9,5},{1... | collective-permute-start | bytes 1794056 | tf_op jit(solution)/shard_map/ppermute | solution.py:423
  61.0 19.2 %collective-permute-start.7 = (bf16[2,1168,128]{2,1,0:T(8,128)(2,1)S(1)}, bf16[2,1168,128]{2,1,0:T(8,128)(2,1)}, u32[]{:S(2)}, u32[]{:S(2)}) collective-permute-start(bf16[2,1168,128]{2,1,0:T(8,128)(2,1)S(1)} %pad_maximum_fusion.2.refs_1_), channel_id=1, source_target_pairs={{0,4},{1,5},{2,6},{3,7},{4,8},{5,9},{6,10},{7,11},{8,12},{9,13},{1... | collective-permute-start | bytes 1794056 | tf_op jit(solution)/shard_map/ppermute | solution.py:423
  64.2 18.4 %collective-permute-start.10 = (bf16[2,1168,128]{2,1,0:T(8,128)(2,1)}, bf16[2,1168,128]{2,1,0:T(8,128)(2,1)S(1)}, u32[]{:S(2)}, u32[]{:S(2)}) collective-permute-start(bf16[2,1168,128]{2,1,0:T(8,128)(2,1)} %collective-permute-done.6.refs_2_), channel_id=1, source_target_pairs={{0,4},{1,5},{2,6},{3,7},{4,8},{5,9},{6,10},{7,11},{8,12},{9,13},{1... | collective-permute-start | bytes 1794056 | tf_op jit(solution)/shard_map/ppermute | solution.py:423
  73.8 16.4 %collective-permute-start.16 = (bf16[2,1168,128]{2,1,0:T(8,128)(2,1)}, bf16[2,1168,128]{2,1,0:T(8,128)(2,1)}, u32[]{:S(2)}, u32[]{:S(2)}) collective-permute-start(bf16[2,1168,128]{2,1,0:T(8,128)(2,1)} %collective-permute-done.12.refs_10_), channel_id=1, source_target_pairs={{0,1},{1,2},{2,3},{3,0},{4,5},{5,6},{6,7},{7,4},{8,9},{9,10},{10,1... | collective-permute-start | bytes 1794056 | tf_op jit(solution)/shard_map/ppermute | solution.py:423
  77.0 13.2 %collective-permute-start.17 = (bf16[2,1168,128]{2,1,0:T(8,128)(2,1)}, bf16[2,1168,128]{2,1,0:T(8,128)(2,1)}, u32[]{:S(2)}, u32[]{:S(2)}) collective-permute-start(bf16[2,1168,128]{2,1,0:T(8,128)(2,1)} %collective-permute-done.15.refs_13_), channel_id=1, source_target_pairs={{0,3},{1,0},{2,1},{3,2},{4,7},{5,4},{6,5},{7,6},{8,11},{9,8},{10,9... | collective-permute-start | bytes 1794056 | tf_op jit(solution)/shard_map/ppermute | solution.py:423
  77.3 12.9 %copy-start.5 = (bf16[2,1168,128]{2,1,0:T(8,128)(2,1)}, bf16[2,1168,128]{2,1,0:T(8,128)(2,1)S(1)}, u32[]{:S(2)}) copy-start(bf16[2,1168,128]{2,1,0:T(8,128)(2,1)S(1)} %collective-permute-done.9.refs_5_) | copy-start | bytes 1794052
  77.3 12.9 %collective-permute-start.11 = (bf16[2,1168,128]{2,1,0:T(8,128)(2,1)S(1)}, bf16[2,1168,128]{2,1,0:T(8,128)(2,1)}, u32[]{:S(2)}, u32[]{:S(2)}) collective-permute-start(bf16[2,1168,128]{2,1,0:T(8,128)(2,1)S(1)} %collective-permute-done.9.refs_5_), channel_id=1, source_target_pairs={{0,12},{1,13},{2,14},{3,15},{4,0},{5,1},{6,2},{7,3},{8,4},{9,5},{1... | collective-permute-start | bytes 1794056 | tf_op jit(solution)/shard_map/ppermute | solution.py:423
  79.6 16.1 %copy-start.7 = (s32[32]{0:T(128)}, s32[32]{0:T(128)S(1)}, u32[]{:S(2)}) copy-start(s32[32]{0:T(128)S(1)} %reshape.309.off_ref) | copy-start | bytes 388
  82.6 7.7 %copy-start.6 = (bf16[2,1168,128]{2,1,0:T(8,128)(2,1)}, bf16[2,1168,128]{2,1,0:T(8,128)(2,1)S(1)}, u32[]{:S(2)}) copy-start(bf16[2,1168,128]{2,1,0:T(8,128)(2,1)S(1)} %collective-permute-done.10.refs_6_) | copy-start | bytes 1794052
  92.5 9.4 %collective-permute-start.18 = (bf16[144,128]{1,0:T(8,128)(2,1)}, bf16[144,128]{1,0:T(8,128)(2,1)S(1)}, u32[]{:S(2)}, u32[]{:S(2)}) collective-permute-start(bf16[144,128]{1,0:T(8,128)(2,1)} %get-tuple-element.31), channel_id=1, source_target_pairs={{0,16},{16,0},{32,48},{48,32},{64,80},{80,64},{96,112},{112,96},{1... | collective-permute-start | bytes 110600 | tf_op jit(solution)/shard_map/ppermute | solution.py:487
  101.9 0.6 copy-start.10
where the time goes:
time: 109 us; the launch traced here: 108 us
  Pallas kernels  42.2 us (39%)
  waiting for transfers between devices  33.9 us (31%)
  starting transfers between devices  25.3 us (23%)
  other arithmetic  4.18 us (4%)
  local copies, waits for them, and re-layouts  2.01 us (2%)
    ppermute x18, waiting for transfers between devices, shifted(): return lax.ppermute(x, 'col', route)  33.9 us
    ppermute x18, starting transfers between devices, shifted(): return lax.ppermute(x, 'col', route)  22.2 us
    pallas_call x1, Pallas kernels, diag_part(): pl.pallas_call(diag_kernel, grid=(1,), in_specs=[pl.BlockSpec((leaves, 1,...  21.6 us
    pallas_call x1, Pallas kernels, own_part(): pl.pallas_call(own_kernel, in_specs=[SMEM, HBM] + [VMEM] * len(pays), out...  6.25 us
    pallas_call x1, Pallas kernels, near_part(): pl.pallas_call(near_kernel, in_specs=[SMEM, SMEM, SMEM, VMEM, HBM] + [HBM...  6.16 us
    pallas_call x1, Pallas kernels, top_part(): pl.pallas_call(top_kernel, out_shape=[shape, shape], scratch_shapes=[pltp...  5.99 us
    ppermute x1, starting transfers between devices, local(): lax.ppermute(outgoing, 'row', [(r, r ^ 1) for r in range(row_count)])  3.18 us
    pallas_call x1, Pallas kernels, pick_part(): pl.pallas_call(pick_kernel, in_specs=[SMEM] + [HBM] * len(pieces), out_sh...  2.18 us
  transfers between devices with their start and end apart: 19, of which 8 were waited for; matrix products, arithmetic and copies ran while one was open for 5% of the time, Pallas kernels for 11%

commit v1 on v0

--- a/solution.py
+++ b/solution.py
@@ -308,79 +308,7 @@
     )(counts, near_blocks, *pays)
 
 
-def near_kernel(off_ref, spot_ref, cnt_ref, schur_ref, g_hbm, *refs):
-    pieces, (out_ref, g_buf, r_buf, g_sem, r_sem) = refs[:-5], refs[-5:]
-    leaves, slots = out_ref.shape[:2]
-    rows = r_buf.shape[2]
-    half = len(pieces) // 2
-    count = pieces[0].shape[0]
-
-    def load(i, t):
-        return pltpu.make_async_copy(g_hbm.at[i, t], g_buf.at[i, t], g_sem.at[i, t])
-
-    def fetch(i, t, piece, at):
-        return pltpu.make_async_copy(piece.at[at, pl.ds(0, rows)], r_buf.at[i, t], r_sem.at[i, t])
-
-    for i in range(leaves):
-
-        def begin(t, _, i=i):
-            load(i, t).start()
-            at = i * slots + t
-            spot = spot_ref[at]
-            number = lax.rem(off_ref[at], 2) * half + lax.div(spot, count)
-            for p, piece in enumerate(pieces):
-
-                @pl.when(number == p)
-                def _(piece=piece):
-                    fetch(i, t, piece, lax.rem(spot, count)).start()
-
-        lax.fori_loop(1, cnt_ref[i], begin, None)
-    size = rows // 2
-    for i in range(leaves):
-
-        def some(c, _, i=i):
-            for t in [c * STEP + u for u in range(STEP)]:
-
-                @pl.when((t > 0) & (t < cnt_ref[i]))
-                def _(t=t):
-                    load(i, t).wait()
-                    fetch(i, t, pieces[0], 0).wait()
-
-            for t in [c * STEP + u for u in range(STEP)]:
-                s_j = r_buf[i, t, :size]
-                both = dot(g_buf[i, t, :2].reshape(2 * LANE, size), s_j)
-                value = both[:LANE] + both[LANE:] - dot(g_buf[i, t, 2], r_buf[i, t, size:])
-                out_ref[i, t] = jnp.where(t < cnt_ref[i], value, 0.0)
-
-        def dead(t, _, i=i):
-            out_ref[i, t] = jnp.zeros(out_ref.shape[2:], F32)
-
-        steps = (cnt_ref[i] + (STEP - 1)) // STEP
-        lax.fori_loop(0, steps, some, None)
-        lax.fori_loop(steps * STEP, slots, dead, None)
-        out_ref[i, 0] = schur_ref[i]
-
-
-def near_part(offsets, spots, counts, schur, g, pieces):
-    leaves, slots, _, _, size = g.shape
-    return pl.pallas_call(
-        near_kernel,
-        in_specs=[SMEM, SMEM, SMEM, VMEM, HBM] + [HBM] * len(pieces),
-        out_specs=VMEM,
-        out_shape=jax.ShapeDtypeStruct((leaves, slots, LANE, LANE), F32),
-        scratch_shapes=[
-            pltpu.VMEM(g.shape, BF16),
-            pltpu.VMEM((leaves, slots, 2 * size, LANE), BF16),
-            pltpu.SemaphoreType.DMA((leaves, slots)),
-            pltpu.SemaphoreType.DMA((leaves, slots)),
-        ],
-        compiler_params=LARGE,
-        cost_estimate=guess(6),
-        name="near",
-    )(offsets, spots, counts, schur, g, *pieces)
-
-
-def top_kernel(first_ref, second_ref, far_ref, v_ref, factor_ref, top_ref, w_ref, t_ref):
+def parent(first_ref, second_ref, far_ref, v_ref, factor_ref, top_ref, w_ref, t_ref):
     n = LANE
     row = lax.broadcasted_iota(jnp.int32, (n, n), 0)
     col = lax.broadcasted_iota(jnp.int32, (n, n), 1)
@@ -403,16 +331,80 @@
     factor_ref[0] = jnp.where(row <= col, w_ref[...], 0.0).T
 
 
-def top_part(first, second, far, basis):
+def near_kernel(off_ref, spot_ref, cnt_ref, schur_ref, g_hbm, first_ref, second_ref, far_ref, v_ref, *refs):
+    pieces, (out_ref, factor_ref, top_ref, g_buf, r_buf, w_ref, t_ref, g_sem, r_sem) = refs[:-9], refs[-9:]
+    leaves, slots = out_ref.shape[:2]
+    rows = r_buf.shape[2]
+    half = len(pieces) // 2
+    count = pieces[0].shape[0]
+
+    def load(i, t):
+        return pltpu.make_async_copy(g_hbm.at[i, t], g_buf.at[i, t], g_sem.at[i, t])
+
+    def fetch(i, t, piece, at):
+        return pltpu.make_async_copy(piece.at[at, pl.ds(0, rows)], r_buf.at[i, t], r_sem.at[i, t])
+
+    for i in range(leaves):
+
+        def begin(t, _, i=i):
+            load(i, t).start()
+            at = i * slots + t
+            spot = spot_ref[at]
+            number = lax.rem(off_ref[at], 2) * half + lax.div(spot, count)
+            for p, piece in enumerate(pieces):
+
+                @pl.when(number == p)
+                def _(piece=piece):
+                    fetch(i, t, piece, lax.rem(spot, count)).start()
+
+        lax.fori_loop(1, cnt_ref[i], begin, None)
+    parent(first_ref, second_ref, far_ref, v_ref, factor_ref, top_ref, w_ref, t_ref)
+    size = rows // 2
+    for i in range(leaves):
+
+        def some(c, _, i=i):
+            for t in [c * STEP + u for u in range(STEP)]:
+
+                @pl.when((t > 0) & (t < cnt_ref[i]))
+                def _(t=t):
+                    load(i, t).wait()
+                    fetch(i, t, pieces[0], 0).wait()
+
+            for t in [c * STEP + u for u in range(STEP)]:
+                s_j = r_buf[i, t, :size]
+                both = dot(g_buf[i, t, :2].reshape(2 * LANE, size), s_j)
+                value = both[:LANE] + both[LANE:] - dot(g_buf[i, t, 2], r_buf[i, t, size:])
+                out_ref[i, t] = jnp.where(t < cnt_ref[i], value, 0.0)
+
+        def dead(t, _, i=i):
+            out_ref[i, t] = jnp.zeros(out_ref.shape[2:], F32)
+
+        steps = (cnt_ref[i] + (STEP - 1)) // STEP
+        lax.fori_loop(0, steps, some, None)
+        lax.fori_loop(steps * STEP, slots, dead, None)
+        out_ref[i, 0] = schur_ref[i]
+
+
+def near_part(offsets, spots, counts, schur, g, first, second, far, basis, pieces):
+    leaves, slots, _, _, size = g.shape
     shape = jax.ShapeDtypeStruct((1, LANE, LANE), F32)
     return pl.pallas_call(
-        top_kernel,
-        out_shape=[shape, shape],
-        scratch_shapes=[pltpu.VMEM((LANE, LANE), F32), pltpu.VMEM((LANE, LANE), F32)],
+        near_kernel,
+        in_specs=[SMEM, SMEM, SMEM, VMEM, HBM, VMEM, VMEM, VMEM, VMEM] + [HBM] * len(pieces),
+        out_specs=[VMEM, VMEM, VMEM],
+        out_shape=[jax.ShapeDtypeStruct((leaves, slots, LANE, LANE), F32), shape, shape],
+        scratch_shapes=[
+            pltpu.VMEM(g.shape, BF16),
+            pltpu.VMEM((leaves, slots, 2 * size, LANE), BF16),
+            pltpu.VMEM((LANE, LANE), F32),
+            pltpu.VMEM((LANE, LANE), F32),
+            pltpu.SemaphoreType.DMA((leaves, slots)),
+            pltpu.SemaphoreType.DMA((leaves, slots)),
+        ],
         compiler_params=LARGE,
-        cost_estimate=guess(8),
-        name="top",
-    )(first, second, far, basis)
+        cost_estimate=guess(12),
+        name="near",
+    )(offsets, spots, counts, schur, g, first, second, far, basis, *pieces)
 
 
 def shifted(x, side, step_z, step_x):
@@ -485,8 +477,9 @@
         pieces += [shift(low_far[k][0], 1), shift(high_far[k][1], -1)]
     first, outgoing = pick_part(where, pieces)
     second = lax.ppermute(outgoing, "row", [(r, r ^ 1) for r in range(row_count)])
-    near_schur = near_part(offsets, spots, near_count, schur, g, pieces)
-    top_factor, top_schur = top_part(first, second, far_coupling, parent_basis)
+    near_schur, top_factor, top_schur = near_part(
+        offsets, spots, near_count, schur, g, first, second, far_coupling, parent_basis, pieces
+    )
     return factors, near_schur, top_factor, top_schur
 
 

time: 109 us -> 108 us (level)
  Pallas kernels: 42.2 us -> 39.7 us
  starting transfers between devices: 25.3 us -> 27.6 us
  waiting for transfers between devices: 33.9 us -> 32.4 us
    pallas_call x2 -> x1, Pallas kernels: 12.1 us -> 9.69 us  [near_part(): pl.pallas_call(near_kernel, in_specs=[SMEM, SMEM, SMEM, VMEM, HBM, VMEM,...]
    ppermute x18, starting transfers between devices: 22.2 us -> 24.5 us  [shifted(): return lax.ppermute(x, 'col', route)]
    ppermute x18, waiting for transfers between devices: 33.9 us -> 31.9 us  [shifted(): return lax.ppermute(x, 'col', route)]
  transfers between devices with their start and end apart: 19 -> 19, of which waited for: 8 -> 9; matrix products, arithmetic and copies ran while one was open for 5% -> 5% of each run, Pallas kernels for 11% -> 6%
where the time goes in v1:
time: 108 us; the launch traced here: 107 us
  Pallas kernels  39.7 us (37%)
  waiting for transfers between devices  32.4 us (30%)
  starting transfers between devices  27.6 us (26%)
  other arithmetic  4.17 us (4%)
  local copies, waits for them, and re-layouts  2.01 us (2%)
    ppermute x18, waiting for transfers between devices, shifted(): return lax.ppermute(x, 'col', route)  31.9 us
    ppermute x18, starting transfers between devices, shifted(): return lax.ppermute(x, 'col', route)  24.5 us
    pallas_call x1, Pallas kernels, diag_part(): pl.pallas_call(diag_kernel, grid=(1,), in_specs=[pl.BlockSpec((leaves, 1,...  21.6 us
    pallas_call x1, Pallas kernels, near_part(): pl.pallas_call(near_kernel, in_specs=[SMEM, SMEM, SMEM, VMEM, HBM, VMEM,...  9.69 us
    pallas_call x1, Pallas kernels, own_part(): pl.pallas_call(own_kernel, in_specs=[SMEM, HBM] + [VMEM] * len(pays), out...  6.26 us
    ppermute x1, starting transfers between devices, local(): lax.ppermute(outgoing, 'row', [(r, r ^ 1) for r in range(row_count)])  3.06 us
    pallas_call x1, Pallas kernels, pick_part(): pl.pallas_call(pick_kernel, in_specs=[SMEM] + [HBM] * len(pieces), out_sh...  2.2 us
  transfers between devices with their start and end apart: 19, of which 9 were waited for; matrix products, arithmetic and copies ran while one was open for 5% of the time, Pallas kernels for 6%

profile of v1, /device:TPU:1, one launch (start us, length us, event | category | flops | bytes accessed | tf_op | source)
XLA Modules:
  0.0 106.9 jit_solution(10857230305701214346)
XLA Ops:
  0.6 21.6 %diag.1 = (f32[2,384,384]{2,1,0:T(8,128)}, f32[2,128,128]{2,1,0:T(8,128)}, bf16[1168,128]{1,0:T(8,128)(2,1)}, bf16[1168,128]{1,0:T(8,128)(2,1)}) custom-call(bf16[2,16,512,512]{3,2,1,0:T(8,128)(2,1)} %a_hbm.1, bf16[2,512,512]{2,1,0:T(8,128)(2,1)} %u_ref.1), custom_call_target="tpu_custom_call" | custom-call | flops 25999998976 | tf_op jit(solution)/shard_map/diag/pallas_call | solution.py:186
  22.2 2.0 %collective-permute-start = (bf16[1168,128]{1,0:T(8,128)(2,1)}, bf16[1168,128]{1,0:T(8,128)(2,1)S(1)}, u32[]{:S(2)}, u32[]{:S(2)}) collective-permute-start(bf16[1168,128]{1,0:T(8,128)(2,1)} %get-tuple-element.24.refs_0_), channel_id=1, source_target_pairs={{0,1},{1,2},{2,3},{3,0},{4,5},{5,6},{6,7},{7,4},{8,9},{9,10},{10,1... | collective-permute-start | bytes 897032 | tf_op jit(solution)/shard_map/ppermute | solution.py:415
  24.2 1.6 %collective-permute-start.1 = (bf16[1168,128]{1,0:T(8,128)(2,1)}, bf16[1168,128]{1,0:T(8,128)(2,1)S(1)}, u32[]{:S(2)}, u32[]{:S(2)}) collective-permute-start(bf16[1168,128]{1,0:T(8,128)(2,1)} %get-tuple-element.25.refs_1_), channel_id=1, source_target_pairs={{0,4},{1,5},{2,6},{3,7},{4,8},{5,9},{6,10},{7,11},{8,12},{9,13},{1... | collective-permute-start | bytes 897032 | tf_op jit(solution)/shard_map/ppermute | solution.py:415
  25.9 1.5 %collective-permute-start.2 = (bf16[1168,128]{1,0:T(8,128)(2,1)}, bf16[1168,128]{1,0:T(8,128)(2,1)S(1)}, u32[]{:S(2)}, u32[]{:S(2)}) collective-permute-start(bf16[1168,128]{1,0:T(8,128)(2,1)} %get-tuple-element.24.refs_0_), channel_id=1, source_target_pairs={{0,3},{1,0},{2,1},{3,2},{4,7},{5,4},{6,5},{7,6},{8,11},{9,8},{10,9... | collective-permute-start | bytes 897032 | tf_op jit(solution)/shard_map/ppermute | solution.py:415
  27.3 2.1 %collective-permute-start.3 = (bf16[1168,128]{1,0:T(8,128)(2,1)}, bf16[1168,128]{1,0:T(8,128)(2,1)S(1)}, u32[]{:S(2)}, u32[]{:S(2)}) collective-permute-start(bf16[1168,128]{1,0:T(8,128)(2,1)} %get-tuple-element.25.refs_1_), channel_id=1, source_target_pairs={{0,12},{1,13},{2,14},{3,15},{4,0},{5,1},{6,2},{7,3},{8,4},{9,5},{1... | collective-permute-start | bytes 897032 | tf_op jit(solution)/shard_map/ppermute | solution.py:415
  29.5 2.6 %collective-permute-done = bf16[1168,128]{1,0:T(8,128)(2,1)S(1)} collective-permute-done((bf16[1168,128]{1,0:T(8,128)(2,1)}, bf16[1168,128]{1,0:T(8,128)(2,1)S(1)}, u32[]{:S(2)}, u32[]{:S(2)}) %collective-permute-start) | collective-permute-done | bytes 299040 | tf_op jit(solution)/shard_map/ppermute | solution.py:415
  32.1 1.0 pad_maximum_fusion.refs_0_
  33.1 0.0 copy-start
  33.1 4.1 %collective-permute-start.8 = (bf16[2,1168,128]{2,1,0:T(8,128)(2,1)S(1)}, bf16[2,1168,128]{2,1,0:T(8,128)(2,1)S(1)}, u32[]{:S(2)}, u32[]{:S(2)}) collective-permute-start(bf16[2,1168,128]{2,1,0:T(8,128)(2,1)S(1)} %pad_maximum_fusion.refs_0_), channel_id=1, source_target_pairs={{0,12},{1,13},{2,14},{3,15},{4,0},{5,1},{6,2},{7,3},{8,4},{9,5},{1... | collective-permute-start | bytes 1794056 | tf_op jit(solution)/shard_map/ppermute | solution.py:415
  37.3 0.0 collective-permute-start.6
  37.3 0.0 collective-permute-done.1
  37.3 1.0 pad_maximum_fusion.1.refs_8_
  38.3 0.0 copy-start.1
  38.3 0.0 copy-start.9
  38.3 0.0 copy-start.10
  38.3 0.1 collective-permute-start.4
  38.4 0.0 collective-permute-done.3
  38.4 2.7 %collective-permute-start.5 = (bf16[1168,128]{1,0:T(8,128)(2,1)S(1)}, bf16[1168,128]{1,0:T(8,128)(2,1)S(1)}, u32[]{:S(2)}, u32[]{:S(2)}) collective-permute-start(bf16[1168,128]{1,0:T(8,128)(2,1)S(1)} %collective-permute-done.3), channel_id=1, source_target_pairs={{0,12},{1,13},{2,14},{3,15},{4,0},{5,1},{6,2},{7,3},{8,4},{9,5},{1... | collective-permute-start | bytes 897032 | tf_op jit(solution)/shard_map/ppermute | solution.py:415
  41.2 6.3 %own.1.g_hbm = bf16[2,16,3,128,512]{4,3,2,1,0:T(8,128)(2,1)} custom-call(s32[2]{0:T(128)} %cnt_ref.3, bf16[2,16,512,512]{3,2,1,0:T(8,128)(2,1)} %a_hbm.1, bf16[1168,128]{1,0:T(8,128)(2,1)} %get-tuple-element.24.refs_0_, bf16[1168,128]{1,0:T(8,128)(2,1)} %get-tuple-element.25.refs_1_), custom_call_target="tpu_custom_call" | custom-call | flops 8000000000 | tf_op jit(solution)/shard_map/own/pallas_call | solution.py:293
  47.4 0.0 copy-done
  47.4 0.0 collective-permute-done.2
  47.4 2.3 %collective-permute-start.14 = (bf16[2,1168,128]{2,1,0:T(8,128)(2,1)S(1)}, bf16[2,1168,128]{2,1,0:T(8,128)(2,1)S(1)}, u32[]{:S(2)}, u32[]{:S(2)}) collective-permute-start(bf16[2,1168,128]{2,1,0:T(8,128)(2,1)S(1)} %pad_maximum_fusion.1.refs_8_), channel_id=1, source_target_pairs={{0,3},{1,0},{2,1},{3,2},{4,7},{5,4},{6,5},{7,6},{8,11},{9,8},{10,9... | collective-permute-start | bytes 1794056 | tf_op jit(solution)/shard_map/ppermute | solution.py:415
  49.7 0.0 collective-permute-done.4
  49.7 0.0 copy-done.1
  49.7 0.0 collective-permute-start.12
  49.7 5.2 %collective-permute-done.5 = bf16[1168,128]{1,0:T(8,128)(2,1)S(1)} collective-permute-done((bf16[1168,128]{1,0:T(8,128)(2,1)S(1)}, bf16[1168,128]{1,0:T(8,128)(2,1)S(1)}, u32[]{:S(2)}, u32[]{:S(2)}) %collective-permute-start.5) | collective-permute-done | bytes 299040 | tf_op jit(solution)/shard_map/ppermute | solution.py:415
  54.9 0.1 pad_maximum_fusion.3.refs_9_
  55.0 0.0 copy-start.2
  55.0 1.4 %collective-permute-start.15 = (bf16[2,1168,128]{2,1,0:T(8,128)(2,1)S(1)}, bf16[2,1168,128]{2,1,0:T(8,128)(2,1)}, u32[]{:S(2)}, u32[]{:S(2)}) collective-permute-start(bf16[2,1168,128]{2,1,0:T(8,128)(2,1)S(1)} %pad_maximum_fusion.3.refs_9_), channel_id=1, source_target_pairs={{0,3},{1,0},{2,1},{3,2},{4,7},{5,4},{6,5},{7,6},{8,11},{9,8},{10,9... | collective-permute-start | bytes 1794056 | tf_op jit(solution)/shard_map/ppermute | solution.py:415
  56.3 0.1 pad_maximum_fusion.2.refs_1_
  56.4 0.0 copy-start.3
  56.4 0.0 collective-permute-done.8.refs_4_
  56.4 0.0 copy-start.4
  56.4 0.2 collective-permute-start.13
  56.7 0.0 collective-permute-done.6.refs_2_
  56.7 3.5 %collective-permute-start.9 = (bf16[2,1168,128]{2,1,0:T(8,128)(2,1)S(1)}, bf16[2,1168,128]{2,1,0:T(8,128)(2,1)S(1)}, u32[]{:S(2)}, u32[]{:S(2)}) collective-permute-start(bf16[2,1168,128]{2,1,0:T(8,128)(2,1)S(1)} %pad_maximum_fusion.2.refs_1_), channel_id=1, source_target_pairs={{0,12},{1,13},{2,14},{3,15},{4,0},{5,1},{6,2},{7,3},{8,4},{9,5},{1... | collective-permute-start | bytes 1794056 | tf_op jit(solution)/shard_map/ppermute | solution.py:415
  60.2 0.3 collective-permute-done.14.refs_12_
  60.5 0.0 collective-permute-start.7
  60.5 3.2 %collective-permute-done.12.refs_10_ = bf16[2,1168,128]{2,1,0:T(8,128)(2,1)} collective-permute-done((bf16[2,1168,128]{2,1,0:T(8,128)(2,1)S(1)}, bf16[2,1168,128]{2,1,0:T(8,128)(2,1)}, u32[]{:S(2)}, u32[]{:S(2)}) %collective-permute-start.12) | collective-permute-done | bytes 598048 | tf_op jit(solution)/shard_map/ppermute | solution.py:415
  63.8 0.0 collective-permute-start.10
  63.8 9.6 %collective-permute-done.15.refs_13_ = bf16[2,1168,128]{2,1,0:T(8,128)(2,1)} collective-permute-done((bf16[2,1168,128]{2,1,0:T(8,128)(2,1)S(1)}, bf16[2,1168,128]{2,1,0:T(8,128)(2,1)}, u32[]{:S(2)}, u32[]{:S(2)}) %collective-permute-start.15) | collective-permute-done | bytes 598048 | tf_op jit(solution)/shard_map/ppermute | solution.py:415
  73.3 1.8 %collective-permute-start.16 = (bf16[2,1168,128]{2,1,0:T(8,128)(2,1)}, bf16[2,1168,128]{2,1,0:T(8,128)(2,1)}, u32[]{:S(2)}, u32[]{:S(2)}) collective-permute-start(bf16[2,1168,128]{2,1,0:T(8,128)(2,1)} %collective-permute-done.12.refs_10_), channel_id=1, source_target_pairs={{0,1},{1,2},{2,3},{3,0},{4,5},{5,6},{6,7},{7,4},{8,9},{9,10},{10,1... | collective-permute-start | bytes 1794056 | tf_op jit(solution)/shard_map/ppermute | solution.py:415
  75.1 1.5 %collective-permute-done.13.refs_11_ = bf16[2,1168,128]{2,1,0:T(8,128)(2,1)S(1)} collective-permute-done((bf16[2,1168,128]{2,1,0:T(8,128)(2,1)S(1)}, bf16[2,1168,128]{2,1,0:T(8,128)(2,1)S(1)}, u32[]{:S(2)}, u32[]{:S(2)}) %collective-permute-start.13) | collective-permute-done | bytes 598048 | tf_op jit(solution)/shard_map/ppermute | solution.py:415
  76.6 0.4 collective-permute-start.17
  76.9 0.0 collective-permute-done.9.refs_5_
  76.9 0.8 collective-permute-start.11
  77.7 0.0 copy-done.9
  77.7 0.6 constant_dynamic-slice_fusion.1
  78.3 1.4 %compare_select_fusion.14 = (s32[2,1]{0,1:T(1,128)S(1)}, s32[2,1]{0,1:T(1,128)S(1)}) fusion(s32[]{:T(128)S(6)} %select_n.230, s32[]{:T(128)S(6)} %select_n.224, s32[]{:T(128)S(6)} %mul.38, s32[1,1]{0,1:T(1,128)} %get-tuple-element.39, s32[1,1]{0,1:T(1,128)} %get-tuple-element.38), kind=kLoop, calls=%fused_computation.23 | loop fusion | flops 164 | bytes 36 | tf_op jit(solution)/shard_map/jit(_where)/select_n | solution.py:450
  79.7 0.1 copy.11
  79.8 0.6 reshape.310.where_ref
  80.4 0.0 copy-done.10
  80.4 0.1 reshape.309.off_ref
  80.5 0.0 collective-permute-done.7.refs_3_
  80.5 3.1 %collective-permute-done.10.refs_6_ = bf16[2,1168,128]{2,1,0:T(8,128)(2,1)S(1)} collective-permute-done((bf16[2,1168,128]{2,1,0:T(8,128)(2,1)}, bf16[2,1168,128]{2,1,0:T(8,128)(2,1)S(1)}, u32[]{:S(2)}, u32[]{:S(2)}) %collective-permute-start.10) | collective-permute-done | bytes 598048 | tf_op jit(solution)/shard_map/ppermute | solution.py:415
  83.6 6.4 %collective-permute-done.16.refs_14_ = bf16[2,1168,128]{2,1,0:T(8,128)(2,1)} collective-permute-done((bf16[2,1168,128]{2,1,0:T(8,128)(2,1)}, bf16[2,1168,128]{2,1,0:T(8,128)(2,1)}, u32[]{:S(2)}, u32[]{:S(2)}) %collective-permute-start.16) | collective-permute-done | bytes 598048 | tf_op jit(solution)/shard_map/ppermute | solution.py:415
  90.0 0.0 collective-permute-done.17.refs_15_
  90.0 0.0 collective-permute-done.11.refs_7_
  90.1 2.2 %pick.1 = (bf16[144,128]{1,0:T(8,128)(2,1)}, bf16[144,128]{1,0:T(8,128)(2,1)}) custom-call(s32[4]{0:T(128)} %reshape.310.where_ref, bf16[2,1168,128]{2,1,0:T(8,128)(2,1)} %copy-done, bf16[2,1168,128]{2,1,0:T(8,128)(2,1)} %copy-done.3, bf16[2,1168,128]{2,1,0:T(8,128)(2,1)} %collective-permute-done.6.refs_2_, ...), custom_call_target="tpu_custom_call" | custom-call | tf_op jit(solution)/shard_map/pick/pallas_call | solution.py:239
  92.3 3.1 %collective-permute-start.18 = (bf16[144,128]{1,0:T(8,128)(2,1)}, bf16[144,128]{1,0:T(8,128)(2,1)S(1)}, u32[]{:S(2)}, u32[]{:S(2)}) collective-permute-start(bf16[144,128]{1,0:T(8,128)(2,1)} %get-tuple-element.32), channel_id=1, source_target_pairs={{0,16},{16,0},{32,48},{48,32},{64,80},{80,64},{96,112},{112,96},{1... | collective-permute-start | bytes 110600 | tf_op jit(solution)/shard_map/ppermute | solution.py:479
  95.3 0.6 compare_select_fusion.21.spot_ref
  95.9 0.5 collective-permute-done.18.second_ref
  96.4 0.6 copy-done.12
  97.0 9.7 %near.1 = (f32[2,16,128,128]{3,2,1,0:T(8,128)}, f32[1,128,128]{2,1,0:T(8,128)}, f32[1,128,128]{2,1,0:T(8,128)}) custom-call(s32[32]{0:T(128)} %copy-done.11, s32[32]{0:T(128)} %compare_select_fusion.21.spot_ref, s32[2]{0:T(128)} %cnt_ref.3, f32[2,128,128]{2,1,0:T(8,128)} %get-tuple-element.21.schur_ref, bf16[2,16,3,128,512]{4,3,2,1,0:T(8,128)(2,1)} %own.1.g_hbm, ...), custom_call_target="tpu_custom_call" | custom-call | flops 12000000000 | tf_op jit(solution)/shard_map/near/pallas_call | solution.py:391
  (16 shorter events, 0.0 us)
Async XLA Ops:
  22.2 9.9 %collective-permute-start = (bf16[1168,128]{1,0:T(8,128)(2,1)}, bf16[1168,128]{1,0:T(8,128)(2,1)S(1)}, u32[]{:S(2)}, u32[]{:S(2)}) collective-permute-start(bf16[1168,128]{1,0:T(8,128)(2,1)} %get-tuple-element.24.refs_0_), channel_id=1, source_target_pairs={{0,1},{1,2},{2,3},{3,0},{4,5},{5,6},{6,7},{7,4},{8,9},{9,10},{10,1... | collective-permute-start | bytes 897032 | tf_op jit(solution)/shard_map/ppermute | solution.py:415
  24.2 13.0 %collective-permute-start.1 = (bf16[1168,128]{1,0:T(8,128)(2,1)}, bf16[1168,128]{1,0:T(8,128)(2,1)S(1)}, u32[]{:S(2)}, u32[]{:S(2)}) collective-permute-start(bf16[1168,128]{1,0:T(8,128)(2,1)} %get-tuple-element.25.refs_1_), channel_id=1, source_target_pairs={{0,4},{1,5},{2,6},{3,7},{4,8},{5,9},{6,10},{7,11},{8,12},{9,13},{1... | collective-permute-start | bytes 897032 | tf_op jit(solution)/shard_map/ppermute | solution.py:415
  25.9 21.6 %collective-permute-start.2 = (bf16[1168,128]{1,0:T(8,128)(2,1)}, bf16[1168,128]{1,0:T(8,128)(2,1)S(1)}, u32[]{:S(2)}, u32[]{:S(2)}) collective-permute-start(bf16[1168,128]{1,0:T(8,128)(2,1)} %get-tuple-element.24.refs_0_), channel_id=1, source_target_pairs={{0,3},{1,0},{2,1},{3,2},{4,7},{5,4},{6,5},{7,6},{8,11},{9,8},{10,9... | collective-permute-start | bytes 897032 | tf_op jit(solution)/shard_map/ppermute | solution.py:415
  27.3 11.1 %collective-permute-start.3 = (bf16[1168,128]{1,0:T(8,128)(2,1)}, bf16[1168,128]{1,0:T(8,128)(2,1)S(1)}, u32[]{:S(2)}, u32[]{:S(2)}) collective-permute-start(bf16[1168,128]{1,0:T(8,128)(2,1)} %get-tuple-element.25.refs_1_), channel_id=1, source_target_pairs={{0,12},{1,13},{2,14},{3,15},{4,0},{5,1},{6,2},{7,3},{8,4},{9,5},{1... | collective-permute-start | bytes 897032 | tf_op jit(solution)/shard_map/ppermute | solution.py:415
  33.1 14.3 %copy-start = (bf16[2,1168,128]{2,1,0:T(8,128)(2,1)}, bf16[2,1168,128]{2,1,0:T(8,128)(2,1)S(1)}, u32[]{:S(2)}) copy-start(bf16[2,1168,128]{2,1,0:T(8,128)(2,1)S(1)} %pad_maximum_fusion.refs_0_) | copy-start | bytes 1794052
  33.1 23.3 %collective-permute-start.8 = (bf16[2,1168,128]{2,1,0:T(8,128)(2,1)S(1)}, bf16[2,1168,128]{2,1,0:T(8,128)(2,1)S(1)}, u32[]{:S(2)}, u32[]{:S(2)}) collective-permute-start(bf16[2,1168,128]{2,1,0:T(8,128)(2,1)S(1)} %pad_maximum_fusion.refs_0_), channel_id=1, source_target_pairs={{0,12},{1,13},{2,14},{3,15},{4,0},{5,1},{6,2},{7,3},{8,4},{9,5},{1... | collective-permute-start | bytes 1794056 | tf_op jit(solution)/shard_map/ppermute | solution.py:415
  37.3 19.4 %collective-permute-start.6 = (bf16[2,1168,128]{2,1,0:T(8,128)(2,1)S(1)}, bf16[2,1168,128]{2,1,0:T(8,128)(2,1)}, u32[]{:S(2)}, u32[]{:S(2)}) collective-permute-start(bf16[2,1168,128]{2,1,0:T(8,128)(2,1)S(1)} %pad_maximum_fusion.refs_0_), channel_id=1, source_target_pairs={{0,4},{1,5},{2,6},{3,7},{4,8},{5,9},{6,10},{7,11},{8,12},{9,13},{1... | collective-permute-start | bytes 1794056 | tf_op jit(solution)/shard_map/ppermute | solution.py:415
  38.3 11.4 %copy-start.1 = (bf16[2,1168,128]{2,1,0:T(8,128)(2,1)}, bf16[2,1168,128]{2,1,0:T(8,128)(2,1)S(1)}, u32[]{:S(2)}) copy-start(bf16[2,1168,128]{2,1,0:T(8,128)(2,1)S(1)} %pad_maximum_fusion.1.refs_8_) | copy-start | bytes 1794052
  38.3 39.4 %copy-start.9 = (s32[128,2]{0,1:T(2,128)S(1)}, s32[128,2]{0,1:T(2,128)}, u32[]{:S(2)}) copy-start(s32[128,2]{0,1:T(2,128)} %param.11) | copy-start | bytes 3076
  38.3 42.1 %copy-start.10 = (s32[2,16]{1,0:T(2,128)S(1)}, s32[2,16]{1,0:T(2,128)}, u32[]{:S(2)}) copy-start(s32[2,16]{1,0:T(2,128)} %param.9) | copy-start | bytes 388
  38.3 11.4 %collective-permute-start.4 = (bf16[1168,128]{1,0:T(8,128)(2,1)S(1)}, bf16[1168,128]{1,0:T(8,128)(2,1)S(1)}, u32[]{:S(2)}, u32[]{:S(2)}) collective-permute-start(bf16[1168,128]{1,0:T(8,128)(2,1)S(1)} %collective-permute-done), channel_id=1, source_target_pairs={{0,1},{1,2},{2,3},{3,0},{4,5},{5,6},{6,7},{7,4},{8,9},{9,10},{10,1... | collective-permute-start | bytes 897032 | tf_op jit(solution)/shard_map/ppermute | solution.py:415
  38.4 16.5 %collective-permute-start.5 = (bf16[1168,128]{1,0:T(8,128)(2,1)S(1)}, bf16[1168,128]{1,0:T(8,128)(2,1)S(1)}, u32[]{:S(2)}, u32[]{:S(2)}) collective-permute-start(bf16[1168,128]{1,0:T(8,128)(2,1)S(1)} %collective-permute-done.3), channel_id=1, source_target_pairs={{0,12},{1,13},{2,14},{3,15},{4,0},{5,1},{6,2},{7,3},{8,4},{9,5},{1... | collective-permute-start | bytes 897032 | tf_op jit(solution)/shard_map/ppermute | solution.py:415
  47.4 13.1 %collective-permute-start.14 = (bf16[2,1168,128]{2,1,0:T(8,128)(2,1)S(1)}, bf16[2,1168,128]{2,1,0:T(8,128)(2,1)S(1)}, u32[]{:S(2)}, u32[]{:S(2)}) collective-permute-start(bf16[2,1168,128]{2,1,0:T(8,128)(2,1)S(1)} %pad_maximum_fusion.1.refs_8_), channel_id=1, source_target_pairs={{0,3},{1,0},{2,1},{3,2},{4,7},{5,4},{6,5},{7,6},{8,11},{9,8},{10,9... | collective-permute-start | bytes 1794056 | tf_op jit(solution)/shard_map/ppermute | solution.py:415
  49.7 14.0 %collective-permute-start.12 = (bf16[2,1168,128]{2,1,0:T(8,128)(2,1)S(1)}, bf16[2,1168,128]{2,1,0:T(8,128)(2,1)}, u32[]{:S(2)}, u32[]{:S(2)}) collective-permute-start(bf16[2,1168,128]{2,1,0:T(8,128)(2,1)S(1)} %pad_maximum_fusion.1.refs_8_), channel_id=1, source_target_pairs={{0,1},{1,2},{2,3},{3,0},{4,5},{5,6},{6,7},{7,4},{8,9},{9,10},{10,1... | collective-permute-start | bytes 1794056 | tf_op jit(solution)/shard_map/ppermute | solution.py:415
  55.0 35.0 %copy-start.2 = (bf16[2,1168,128]{2,1,0:T(8,128)(2,1)}, bf16[2,1168,128]{2,1,0:T(8,128)(2,1)S(1)}, u32[]{:S(2)}) copy-start(bf16[2,1168,128]{2,1,0:T(8,128)(2,1)S(1)} %pad_maximum_fusion.3.refs_9_) | copy-start | bytes 1794052
  55.0 18.4 %collective-permute-start.15 = (bf16[2,1168,128]{2,1,0:T(8,128)(2,1)S(1)}, bf16[2,1168,128]{2,1,0:T(8,128)(2,1)}, u32[]{:S(2)}, u32[]{:S(2)}) collective-permute-start(bf16[2,1168,128]{2,1,0:T(8,128)(2,1)S(1)} %pad_maximum_fusion.3.refs_9_), channel_id=1, source_target_pairs={{0,3},{1,0},{2,1},{3,2},{4,7},{5,4},{6,5},{7,6},{8,11},{9,8},{10,9... | collective-permute-start | bytes 1794056 | tf_op jit(solution)/shard_map/ppermute | solution.py:415
  56.4 33.6 %copy-start.3 = (bf16[2,1168,128]{2,1,0:T(8,128)(2,1)}, bf16[2,1168,128]{2,1,0:T(8,128)(2,1)S(1)}, u32[]{:S(2)}) copy-start(bf16[2,1168,128]{2,1,0:T(8,128)(2,1)S(1)} %pad_maximum_fusion.2.refs_1_) | copy-start | bytes 1794052
  56.4 33.6 %copy-start.4 = (bf16[2,1168,128]{2,1,0:T(8,128)(2,1)}, bf16[2,1168,128]{2,1,0:T(8,128)(2,1)S(1)}, u32[]{:S(2)}) copy-start(bf16[2,1168,128]{2,1,0:T(8,128)(2,1)S(1)} %collective-permute-done.8.refs_4_) | copy-start | bytes 1794052
  56.4 20.1 %collective-permute-start.13 = (bf16[2,1168,128]{2,1,0:T(8,128)(2,1)S(1)}, bf16[2,1168,128]{2,1,0:T(8,128)(2,1)S(1)}, u32[]{:S(2)}, u32[]{:S(2)}) collective-permute-start(bf16[2,1168,128]{2,1,0:T(8,128)(2,1)S(1)} %pad_maximum_fusion.3.refs_9_), channel_id=1, source_target_pairs={{0,1},{1,2},{2,3},{3,0},{4,5},{5,6},{6,7},{7,4},{8,9},{9,10},{10,1... | collective-permute-start | bytes 1794056 | tf_op jit(solution)/shard_map/ppermute | solution.py:415
  56.7 20.3 %collective-permute-start.9 = (bf16[2,1168,128]{2,1,0:T(8,128)(2,1)S(1)}, bf16[2,1168,128]{2,1,0:T(8,128)(2,1)S(1)}, u32[]{:S(2)}, u32[]{:S(2)}) collective-permute-start(bf16[2,1168,128]{2,1,0:T(8,128)(2,1)S(1)} %pad_maximum_fusion.2.refs_1_), channel_id=1, source_target_pairs={{0,12},{1,13},{2,14},{3,15},{4,0},{5,1},{6,2},{7,3},{8,4},{9,5},{1... | collective-permute-start | bytes 1794056 | tf_op jit(solution)/shard_map/ppermute | solution.py:415
  60.5 16.4 %copy-start.5 = (bf16[2,1168,128]{2,1,0:T(8,128)(2,1)}, bf16[2,1168,128]{2,1,0:T(8,128)(2,1)S(1)}, u32[]{:S(2)}) copy-start(bf16[2,1168,128]{2,1,0:T(8,128)(2,1)S(1)} %collective-permute-done.14.refs_12_) | copy-start | bytes 1794052
  60.5 20.0 %collective-permute-start.7 = (bf16[2,1168,128]{2,1,0:T(8,128)(2,1)S(1)}, bf16[2,1168,128]{2,1,0:T(8,128)(2,1)}, u32[]{:S(2)}, u32[]{:S(2)}) collective-permute-start(bf16[2,1168,128]{2,1,0:T(8,128)(2,1)S(1)} %pad_maximum_fusion.2.refs_1_), channel_id=1, source_target_pairs={{0,4},{1,5},{2,6},{3,7},{4,8},{5,9},{6,10},{7,11},{8,12},{9,13},{1... | collective-permute-start | bytes 1794056 | tf_op jit(solution)/shard_map/ppermute | solution.py:415
  63.8 19.9 %collective-permute-start.10 = (bf16[2,1168,128]{2,1,0:T(8,128)(2,1)}, bf16[2,1168,128]{2,1,0:T(8,128)(2,1)S(1)}, u32[]{:S(2)}, u32[]{:S(2)}) collective-permute-start(bf16[2,1168,128]{2,1,0:T(8,128)(2,1)} %collective-permute-done.6.refs_2_), channel_id=1, source_target_pairs={{0,4},{1,5},{2,6},{3,7},{4,8},{5,9},{6,10},{7,11},{8,12},{9,13},{1... | collective-permute-start | bytes 1794056 | tf_op jit(solution)/shard_map/ppermute | solution.py:415
  73.3 16.7 %collective-permute-start.16 = (bf16[2,1168,128]{2,1,0:T(8,128)(2,1)}, bf16[2,1168,128]{2,1,0:T(8,128)(2,1)}, u32[]{:S(2)}, u32[]{:S(2)}) collective-permute-start(bf16[2,1168,128]{2,1,0:T(8,128)(2,1)} %collective-permute-done.12.refs_10_), channel_id=1, source_target_pairs={{0,1},{1,2},{2,3},{3,0},{4,5},{5,6},{6,7},{7,4},{8,9},{9,10},{10,1... | collective-permute-start | bytes 1794056 | tf_op jit(solution)/shard_map/ppermute | solution.py:415
  76.6 1.1 %copy-start.6 = (bf16[2,1168,128]{2,1,0:T(8,128)(2,1)}, bf16[2,1168,128]{2,1,0:T(8,128)(2,1)S(1)}, u32[]{:S(2)}) copy-start(bf16[2,1168,128]{2,1,0:T(8,128)(2,1)S(1)} %collective-permute-done.13.refs_11_) | copy-start | bytes 1794052
  76.6 13.4 %collective-permute-start.17 = (bf16[2,1168,128]{2,1,0:T(8,128)(2,1)}, bf16[2,1168,128]{2,1,0:T(8,128)(2,1)}, u32[]{:S(2)}, u32[]{:S(2)}) collective-permute-start(bf16[2,1168,128]{2,1,0:T(8,128)(2,1)} %collective-permute-done.15.refs_13_), channel_id=1, source_target_pairs={{0,3},{1,0},{2,1},{3,2},{4,7},{5,4},{6,5},{7,6},{8,11},{9,8},{10,9... | collective-permute-start | bytes 1794056 | tf_op jit(solution)/shard_map/ppermute | solution.py:415
  76.9 13.1 %copy-start.7 = (bf16[2,1168,128]{2,1,0:T(8,128)(2,1)}, bf16[2,1168,128]{2,1,0:T(8,128)(2,1)S(1)}, u32[]{:S(2)}) copy-start(bf16[2,1168,128]{2,1,0:T(8,128)(2,1)S(1)} %collective-permute-done.9.refs_5_) | copy-start | bytes 1794052
  76.9 13.1 %collective-permute-start.11 = (bf16[2,1168,128]{2,1,0:T(8,128)(2,1)S(1)}, bf16[2,1168,128]{2,1,0:T(8,128)(2,1)}, u32[]{:S(2)}, u32[]{:S(2)}) collective-permute-start(bf16[2,1168,128]{2,1,0:T(8,128)(2,1)S(1)} %collective-permute-done.9.refs_5_), channel_id=1, source_target_pairs={{0,12},{1,13},{2,14},{3,15},{4,0},{5,1},{6,2},{7,3},{8,4},{9,5},{1... | collective-permute-start | bytes 1794056 | tf_op jit(solution)/shard_map/ppermute | solution.py:415
  80.5 15.9 %copy-start.11 = (s32[32]{0:T(128)}, s32[32]{0:T(128)S(1)}, u32[]{:S(2)}) copy-start(s32[32]{0:T(128)S(1)} %reshape.309.off_ref) | copy-start | bytes 388
  83.6 6.4 %copy-start.8 = (bf16[2,1168,128]{2,1,0:T(8,128)(2,1)}, bf16[2,1168,128]{2,1,0:T(8,128)(2,1)S(1)}, u32[]{:S(2)}) copy-start(bf16[2,1168,128]{2,1,0:T(8,128)(2,1)S(1)} %collective-permute-done.10.refs_6_) | copy-start | bytes 1794052
  92.3 4.1 %collective-permute-start.18 = (bf16[144,128]{1,0:T(8,128)(2,1)}, bf16[144,128]{1,0:T(8,128)(2,1)S(1)}, u32[]{:S(2)}, u32[]{:S(2)}) collective-permute-start(bf16[144,128]{1,0:T(8,128)(2,1)} %get-tuple-element.32), channel_id=1, source_target_pairs={{0,16},{16,0},{32,48},{48,32},{64,80},{80,64},{96,112},{112,96},{1... | collective-permute-start | bytes 110600 | tf_op jit(solution)/shard_map/ppermute | solution.py:479
  96.4 0.6 copy-start.12
